TPU v7x, 512 devices: a whole 4x4x16 slice. The times are simulated.
512 devices in a mesh: row: 16 (over x, y), col: 32 (over z, core).
Axes of the slice: x: 4, y: 4, z: 16, core: 2. Of those that a mesh axis runs over, the one named last changes fastest.
Arguments:
- inputs: bfloat16 [2048, 25600], P('row', 'col'), may hold values from -6 to 6
- out_grads: bfloat16 [2048, 5120], P('col', 'row'), may hold values from -0.125 to 0.125
- weights: bfloat16 [5120, 25600], P('row', 'col'), may hold values from -3 to 3
- momentum: float32 [5120, 25600], P('row', 'col'), may hold values from -13 to 13
- right_factor: float32 [25600, 256], P('col'), may hold values from -6 to 6
Outputs:
- weights_new: float32 [5120, 25600], P('row', 'col')
- momentum_new: float32 [5120, 25600], P('row', 'col')
- factor_new: float32 [25600, 256], P('col')
All inputs are finite; a program needn't handle non-finite values.
Results may differ from a plain program's by a relative error of at most 0.0003.
Values may be sent and summed in bfloat16 or wider, within the bound.
A program may use at most 64 MiB of HBM per device.

v0:
```python
import math

import jax
import jax.numpy as jnp
from jax import lax
from jax.sharding import Mesh
from jax.sharding import PartitionSpec as P

M = 5120
N = 25600
RANK = 256
COL = ("col_0", "col_1")
ROW = ("row_0", "row_1")


mix_rate = 0.95
step_rate = 0.3
weight_decay = 0.1
tiny_eps = 1e-06
highest = lax.Precision.HIGHEST


def laid_out(pieces, dim):
    pieces = jnp.moveaxis(pieces, 0, dim)
    lengths = pieces.shape
    return pieces.reshape(*lengths[:dim], lengths[dim] * lengths[dim + 1], *lengths[dim + 2 :])


def all_blocks(value, axes, sequence):
    pieces = value
    for k in sequence:
        pieces = lax.all_gather(pieces, axes[k])
    done = sequence[::-1]
    back = [done.index(k) for k in range(len(axes))]
    pieces = pieces.transpose(*back, *range(len(axes), pieces.ndim))
    return pieces.reshape(-1, *value.shape)


def gathered_by_axis(value, axes, sequence, dim):
    return laid_out(all_blocks(value, axes, sequence), dim)


def gathered_by_axis_2(value, axes, dim):
    for axis in reversed(axes):
        value = lax.all_gather(value, axis, axis=dim, tiled=True)
    return value


def split_up(value, dim, peers):
    before, after = (value.shape[:dim], value.shape[dim + 1 :])
    return jnp.moveaxis(value.reshape(*before, peers, -1, *after), dim, 0)


def sum_at_owner(value, axis, dim):
    peers = lax.axis_size(axis)
    pieces = lax.all_to_all(split_up(value, dim, peers), axis, 0, 0, tiled=True)
    return jnp.sum(pieces, axis=0)


def filled_up(lines, peers):
    spare = -len(lines) % peers
    return jnp.pad(lines, [(0, spare)] + [(0, 0)] * (lines.ndim - 1))


def from_everyone(value, axis):
    copies = jnp.broadcast_to(value, (lax.axis_size(axis), *value.shape))
    return lax.all_to_all(copies, axis, split_axis=0, concat_axis=0, tiled=True)


def collect(value, axis, dim):
    return laid_out(from_everyone(value, axis), dim)


def nested_sum(value, axes):
    lines = value.reshape(-1, value.shape[-1])
    own = sum_at_owner(filled_up(lines, lax.axis_size(axes)), axes, 0)
    whole = collect(own, axes, 0)
    return whole[: len(lines)].reshape(value.shape)


def of_everyone(value, axis):
    return from_everyone(value, axis).sum(axis=0)


def inner_rows(left_side, right_in):
    return lax.dot_general(left_side, right_in, (((0,), (0,)), ((), ())), precision=highest)


def orthonormal(sketch_rows, gram_total):
    factor_low = jnp.linalg.cholesky(gram_total)
    return jax.scipy.linalg.solve_triangular(factor_low, sketch_rows.T, lower=True).T


def on_device(inputs, out_grads, weights, momentum, right_factor):
    grads_all = gathered_by_axis(out_grads, COL, (0, 1), 0)
    gradient = lax.dot_general(
        grads_all,
        gathered_by_axis_2(inputs, ROW, 0),
        (((0,), (0,)), ((), ())),
        preferred_element_type=jnp.float32,
    )
    moment = momentum + gradient
    sketch_part = jnp.dot(moment, right_factor, precision=highest)
    sketch_rows = nested_sum(sketch_part, COL)
    gram_total = nested_sum(inner_rows(sketch_rows, sketch_rows), ROW)
    basis_rows = orthonormal(sketch_rows, gram_total)
    right_part = inner_rows(moment, basis_rows)
    right_side = nested_sum(right_part, ROW)
    squares = of_everyone(jnp.sum(right_side * right_side, axis=0), COL)
    column_scale = lax.rsqrt(squares / N + tiny_eps)
    factor_new = right_side * column_scale
    momentum_new = moment - (1.0 - mix_rate) * jnp.dot(basis_rows, right_side.T, precision=highest)
    update = jnp.dot(basis_rows, factor_new.T, precision=highest)
    weights_new = (
        weights.astype(jnp.float32) * (1.0 - step_rate * weight_decay)
        - step_rate * math.sqrt(M / RANK) * update
    )
    return (weights_new, momentum_new, factor_new)


def solution(mesh):
    torus = Mesh(mesh.devices.reshape(4, 4, 16, 2), ("row_0", "row_1", "col_0", "col_1"))
    return jax.shard_map(
        on_device,
        mesh=torus,
        in_specs=(P(ROW, COL), P(COL, ROW), P(ROW, COL), P(ROW, COL), P(COL, None)),
        out_specs=(P(ROW, COL), P(ROW, COL), P(COL, None)),
        check_vma=False,
    )
```

profile of v0, /device:TPU:1, one launch (start us, length us, event | category | flops | bytes accessed | tf_op | source)
XLA Modules:
  0.0 361.6 jit_solution(15033897234010282396)
XLA Ops:
  7.2 0.0 copy-start
  7.2 0.0 copy-start.3
  7.2 0.0 all-gather.7.cloned.1.call-start
  7.2 36.6 %all-gather = bf16[1024,320]{1,0:T(8,128)(2,1)} all-gather(bf16[64,320]{1,0:T(8,128)(2,1)} %param.6), channel_id=2, replica_groups=mesh['row_0'=4,'row_1'=4,'col_0'=16,'col_1'=2] {'col_0'}, dimensions={0}, use_global_device_ids=true | all-gather | bytes 696320 | tf_op jit(solution)/shard_map/all_gather | solution.py:32
  43.9 0.0 all-gather.7.cloned.1.call-update
  43.9 0.0 all-gather.5.cloned.1.call-start
  44.0 0.0 copy-done.3
  44.0 12.5 %all_gather.22 = bf16[512,800]{0,1:T(8,128)(2,1)} all-gather(bf16[128,800]{0,1:T(8,128)(2,1)S(1)} %copy-done.3), channel_id=1, replica_groups=mesh['row_0'=4,'row_1'=4,'col_0'=16,'col_1'=2] {'row_1'}, dimensions={0}, use_global_device_ids=true | all-gather | bytes 1024000 | tf_op jit(solution)/shard_map/all_gather | solution.py:45
  56.4 0.0 all-gather.5.cloned.1.call-update
  56.5 12.3 %all-gather.7.cloned.1.call-done = bf16[32,64,320]{2,1,0:T(8,128)(2,1)} async-done(((bf16[16,64,320]{2,1,0:T(8,128)(2,1)}), bf16[32,64,320]{2,1,0:T(8,128)(2,1)}) %all-gather.7.cloned.1.call-update) | async-done | bytes 1310736 | tf_op jit(solution)/shard_map/all_gather | solution.py:32
  68.7 1.6 copy.21
  70.3 48.7 %all-gather.5.cloned.1.call-done = bf16[2048,800]{0,1:T(8,128)(2,1)} async-done(((bf16[512,800]{0,1:T(8,128)(2,1)}), bf16[2048,800]{0,1:T(8,128)(2,1)}) %all-gather.5.cloned.1.call-update) | async-done | bytes 3276816 | tf_op jit(solution)/shard_map/all_gather | solution.py:45
  119.0 4.2 %convolution_add_fusion = f32[320,800]{1,0:T(8,128)S(1)} fusion(f32[320,800]{1,0:T(8,128)} %param.8, bf16[2048,320]{1,0:T(8,128)(2,1)S(1)} %bitcast.55, bf16[2048,800]{0,1:T(8,128)(2,1)} %all-gather.5.cloned.1.call-done), kind=kOutput, calls=%fused_computation.6 | convolution fusion | flops 1048832000 | bytes 6635520 | tf_op jit(solution)/shard_map/dot_general | solution.py:96
  123.2 0.0 copy-done
  123.2 1.2 fusion.15
  124.5 46.4 %all_to_all.36 = f32[32,10,256]{2,1,0:T(8,128)S(1)} all-to-all(f32[32,10,256]{2,1,0:T(8,128)S(1)} %reshape.51), channel_id=1, replica_groups=mesh['row_0'=4,'row_1'=4,'col_0'=16,'col_1'=2] {'col_0','col_1'}, dimensions={0} | all-to-all | bytes 655360 | tf_op jit(solution)/shard_map/all_to_all | solution.py:56
  170.9 0.1 reduce_sum.45
  170.9 0.1 broadcast_in_dim.15
  171.0 36.7 %all_to_all.37 = f32[32,10,256]{2,1,0:T(8,128)S(1)} all-to-all(f32[32,10,256]{2,1,0:T(8,128)S(1)} %broadcast_in_dim.15), channel_id=1, replica_groups=mesh['row_0'=4,'row_1'=4,'col_0'=16,'col_1'=2] {'col_0','col_1'}, dimensions={0} | all-to-all | bytes 655360 | tf_op jit(solution)/shard_map/all_to_all | solution.py:67
  207.7 0.2 copy.22
  207.9 0.6 fusion.16
  208.5 12.6 %all_to_all.38 = f32[16,16,256]{2,1,0:T(8,128)S(1)} all-to-all(f32[16,16,256]{2,1,0:T(8,128)S(1)} %fusion.16), channel_id=1, replica_groups=mesh['row_0'=4,'row_1'=4,'col_0'=16,'col_1'=2] {'row_0','row_1'}, dimensions={0} | all-to-all | bytes 524288 | tf_op jit(solution)/shard_map/all_to_all | solution.py:56
  221.2 0.7 broadcast_in_dim.16
  221.9 3.7 %all-to-all-start.3 = ((f32[16,16,256]{2,1,0:T(8,128)}), f32[16,16,256]{2,1,0:T(8,128)S(1)}, u32[]{:S(2)}, u32[]{:S(2)}) async-start(f32[16,16,256]{2,1,0:T(8,128)} %broadcast_in_dim.16), calls=%async_computation.3 | async-start | bytes 524288 | tf_op jit(solution)/shard_map/all_to_all | solution.py:67
  225.7 7.2 %all-to-all-done.3 = f32[16,16,256]{2,1,0:T(8,128)S(1)} async-done(((f32[16,16,256]{2,1,0:T(8,128)}), f32[16,16,256]{2,1,0:T(8,128)S(1)}, u32[]{:S(2)}, u32[]{:S(2)}) %all-to-all-start.3) | async-done | bytes 262176 | tf_op jit(solution)/shard_map/all_to_all | solution.py:67
  232.9 0.1 copy.23
  233.1 11.7 %cholesky.50 = f32[128,128]{1,0:T(8,128)S(1)} custom-call(f32[128,128]{1,0:T(8,128)S(1)} %cholesky.118), custom_call_target="Cholesky" | custom-call | tf_op jit(solution)/shard_map/jit(cholesky)/cholesky | solution.py:90
  244.9 9.8 %custom-call.15 = f32[1,128,128]{1,2,0:T(8,128)S(1)} custom-call(f32[1,128,128]{2,1,0:T(8,128)S(1)} %get-tuple-element.24), custom_call_target="InvertDiagBlocksLowerTriangular" | custom-call | tf_op jit(solution)/shard_map/jit(cholesky)/cholesky | solution.py:90
  254.7 0.2 constant_dynamic-update-slice_fusion.1
  254.9 0.3 convolution_subtract_fusion.1
  255.2 11.7 %cholesky.105 = f32[128,128]{1,0:T(8,128)S(1)} custom-call(f32[128,128]{1,0:T(8,128)S(1)} %convolution_subtract_fusion.1), custom_call_target="Cholesky" | custom-call | tf_op jit(solution)/shard_map/jit(cholesky)/cholesky | solution.py:90
  266.9 0.6 compare_reduce_fusion
  268.9 0.1 triangular_solve.57
  269.0 4.0 %while.1 = (s32[]{:T(128)}, f32[256,256]{1,0:T(8,128)S(1)}, s32[2,2]{1,0:T(2,128)S(1)}, f32[2,128,128]{2,1,0:T(8,128)S(1)}, s32[]{:T(128)}) while((s32[]{:T(128)}, f32[256,256]{1,0:T(8,128)S(1)}, s32[2,2]{1,0:T(2,128)S(1)}, f32[2,128,128]{2,1,0:T(8,128)S(1)}, s32[]{:T(128)}) %tuple.27), condition=%wide.while_cond, body=%wide.while_body.sunk | while | flops 2 | bytes 131181 | solution.py:91
  269.0 0.6 fusion.31
  269.6 1.4 bitcast_dynamic-update-slice_fusion.2
  271.0 0.6 fusion.31
  271.6 1.4 bitcast_dynamic-update-slice_fusion.2
  273.0 19.9 %custom-call.16 = f32[2,128,128]{1,2,0:T(8,128)S(1)} custom-call(f32[2,128,128]{2,1,0:T(8,128)S(1)} %get-tuple-element.10), custom_call_target="InvertDiagBlocksLowerTriangular" | custom-call | tf_op jit(solution)/shard_map/jit(_solve_triangular)/triangular_solve | solution.py:91
  292.9 0.3 fusion.4
  293.2 0.3 convolution_subtract_fusion
  293.5 0.3 fusion.7
  293.8 2.3 fusion.3
  296.1 1.0 reshape.54
  297.1 15.9 %all_to_all.39 = f32[16,50,256]{2,1,0:T(8,128)S(1)} all-to-all(f32[16,50,256]{2,1,0:T(8,128)} %reshape.54), channel_id=1, replica_groups=mesh['row_0'=4,'row_1'=4,'col_0'=16,'col_1'=2] {'row_0','row_1'}, dimensions={0} | all-to-all | bytes 1638400 | tf_op jit(solution)/shard_map/all_to_all | solution.py:56
  313.0 0.1 reduce_sum.47
  313.1 0.1 broadcast_in_dim.17
  313.2 13.9 %all_to_all.40 = f32[16,50,256]{2,1,0:T(8,128)S(1)} all-to-all(f32[16,50,256]{2,1,0:T(8,128)S(1)} %broadcast_in_dim.17), channel_id=1, replica_groups=mesh['row_0'=4,'row_1'=4,'col_0'=16,'col_1'=2] {'row_0','row_1'}, dimensions={0} | all-to-all | bytes 1638400 | tf_op jit(solution)/shard_map/all_to_all | solution.py:67
  327.0 0.1 multiply_reduce_fusion
  327.2 0.6 broadcast_in_dim.18
  327.8 11.0 %all-to-all-start.6 = ((f32[32,1,256]{2,1,0:T(1,128)}), f32[32,1,256]{2,1,0:T(1,128)S(1)}, u32[]{:S(2)}, u32[]{:S(2)}) async-start(f32[32,1,256]{2,1,0:T(1,128)} %broadcast_in_dim.18), calls=%async_computation.6 | async-start | bytes 65536 | tf_op jit(solution)/shard_map/all_to_all | solution.py:67
  338.8 1.0 reshape.55
  339.8 0.0 copy-start.1
  339.8 3.5 fusion.1
  343.3 7.7 %all-to-all-done.6 = f32[32,1,256]{2,1,0:T(1,128)S(1)} async-done(((f32[32,1,256]{2,1,0:T(1,128)}), f32[32,1,256]{2,1,0:T(1,128)S(1)}, u32[]{:S(2)}, u32[]{:S(2)}) %all-to-all-start.6) | async-done | bytes 32800 | tf_op jit(solution)/shard_map/all_to_all | solution.py:67
  351.0 0.1 reduce_sum.49
  351.0 0.0 copy-done.1
  351.0 0.1 broadcast_multiply_fusion
  351.1 0.0 copy-start.2
  351.1 3.6 %fusion = f32[320,800]{1,0:T(8,128)} fusion(f32[800,256]{1,0:T(8,128)S(1)} %broadcast_multiply_fusion, bf16[320,800]{1,0:T(8,128)(2,1)} %param.7, f32[128,320]{0,1:T(8,128)S(1)} %fusion.7, f32[128,320]{0,1:T(8,128)S(1)} %fusion.4), kind=kOutput, calls=%fused_computation.4 | convolution fusion | flops 787537920 | bytes 2682880 | tf_op jit(solution)/shard_map/dot_general | solution.py:113
  354.7 0.0 copy-done.2
  (15 shorter events, 0.4 us)
Async XLA Ops:
  7.2 116.1 %copy-start = (f32[800,256]{1,0:T(8,128)S(1)}, f32[800,256]{1,0:T(8,128)}, u32[]{:S(2)}) copy-start(f32[800,256]{1,0:T(8,128)} %param.9) | copy-start | bytes 2457604
  7.2 36.8 %copy-start.3 = (bf16[128,800]{0,1:T(8,128)(2,1)S(1)}, bf16[128,800]{0,1:T(8,128)(2,1)}, u32[]{:S(2)}) copy-start(bf16[128,800]{0,1:T(8,128)(2,1)} %param.5) | copy-start | bytes 614404
  7.2 61.5 %all-gather.7.cloned.1.call-start = ((), (), s32[]{:S(2)}) async-start(), calls=%async_computation.8 | async-start | bytes 2359296 | tf_op jit(solution)/shard_map/all_gather | solution.py:32
  43.9 75.1 %all-gather.5.cloned.1.call-start = ((), (), s32[]{:S(2)}) async-start(), calls=%async_computation.7 | async-start | bytes 4096000 | tf_op jit(solution)/shard_map/all_gather | solution.py:45
  221.9 11.0 %all-to-all-start.3 = ((f32[16,16,256]{2,1,0:T(8,128)}), f32[16,16,256]{2,1,0:T(8,128)S(1)}, u32[]{:S(2)}, u32[]{:S(2)}) async-start(f32[16,16,256]{2,1,0:T(8,128)} %broadcast_in_dim.16), calls=%async_computation.3 | async-start | bytes 524288 | tf_op jit(solution)/shard_map/all_to_all | solution.py:67
  327.8 23.2 %all-to-all-start.6 = ((f32[32,1,256]{2,1,0:T(1,128)}), f32[32,1,256]{2,1,0:T(1,128)S(1)}, u32[]{:S(2)}, u32[]{:S(2)}) async-start(f32[32,1,256]{2,1,0:T(1,128)} %broadcast_in_dim.18), calls=%async_computation.6 | async-start | bytes 65536 | tf_op jit(solution)/shard_map/all_to_all | solution.py:67
  339.8 11.2 %copy-start.1 = (f32[800,256]{1,0:T(8,128)S(1)}, f32[800,256]{1,0:T(8,128)}, u32[]{:S(2)}) copy-start(f32[800,256]{1,0:T(8,128)} %reshape.55) | copy-start | bytes 2457604
  351.1 3.7 %copy-start.2 = (f32[800,256]{1,0:T(8,128)}, f32[800,256]{1,0:T(8,128)S(1)}, u32[]{:S(2)}) copy-start(f32[800,256]{1,0:T(8,128)S(1)} %broadcast_multiply_fusion) | copy-start | bytes 2457604
Sparse Core Ops, SparseCore 0:
  44.0 24.6 all-gather.6
  70.8 48.1 all-gather.4
where the time goes:
time: 362 us
  blocking collectives  175 us (48%)
  waiting for transfers between devices  75.9 us (21%)
  other arithmetic  54.3 us (15%)
  matrix products  16.7 us (5%)
  between operations  15.6 us (4%)
  starting transfers between devices  14.9 us (4%)
  local copies, waits for them, and re-layouts  9.59 us (3%)
    all_to_all x3, blocking collectives, sum_at_owner(): pieces = lax.all_to_all(split_up(value, dim, peers), axis, 0, 0, tiled=True)  74.9 us
    all_to_all x2, blocking collectives, from_everyone(): return lax.all_to_all(copies, axis, split_axis=0, concat_axis=0, tiled=True)  50.6 us
    all_gather x1, waiting for transfers between devices, gathered_by_axis_2(): value = lax.all_gather(value, axis, axis=dim, tiled=True)  48.7 us
    all_gather x1, blocking collectives, all_blocks(): pieces = lax.all_gather(pieces, axes[k])  36.6 us
    another operation x6, other arithmetic, orthonormal(): factor_low = jnp.linalg.cholesky(gram_total)  33.9 us
    another operation x3, other arithmetic, orthonormal(): jax.scipy.linalg.solve_triangular(factor_low, sketch_rows.T, lower=True)  19.9 us
    all_to_all x2, waiting for transfers between devices, from_everyone(): return lax.all_to_all(copies, axis, split_axis=0, concat_axis=0, tiled=True)  14.9 us
    all_to_all x2, starting transfers between devices, from_everyone(): return lax.all_to_all(copies, axis, split_axis=0, concat_axis=0, tiled=True)  14.8 us
  transfers between devices with their start and end apart: 4, of which 4 were waited for; matrix products, arithmetic and copies ran while one was open for 2% of the time, Pallas kernels for 0%

commit v1 on v0

v1 whole, which is shorter than its diff:
```python
import functools
import math

import jax
import jax.numpy as jnp
from jax import lax
from jax.experimental import pallas as pl
from jax.experimental.pallas import tpu as pltpu
from jax.sharding import PartitionSpec as P

M = 5120
N = 25600
RANK = 256
TOKENS = 2048

mix_rate = 0.95
step_rate = 0.3
weight_decay = 0.1
tiny_eps = 1e-06
highest = lax.Precision.HIGHEST
MESH = pl.DeviceIdType.MESH
f32 = jnp.float32
bf16 = jnp.bfloat16
VMEM_LIMIT = 56 * 2**20
XY = [(a, b) for a in range(4) for b in range(4) if (a, b) != (0, 0)]


def place():
    r = lax.axis_index("row")
    c = lax.axis_index("col")
    return r // 4, r % 4, c // 2, c % 2


def at(x, y, z, k):
    return (x * 4 + y, z * 2 + k)


def moved(dx=0, dy=0, dz=0, dk=0):
    x, y, z, k = place()
    return at((x + dx) % 4, (y + dy) % 4, (z + dz) % 16, (k + dk) % 2)


def greet(offsets):
    barrier = pltpu.get_barrier_semaphore()
    for o in offsets:
        pl.semaphore_signal(barrier, inc=1, device_id=moved(*o), device_id_type=MESH)
    return lambda: pl.semaphore_wait(barrier, len(offsets))


def send(src, dst, send_sem, recv_sem, to):
    copy = pltpu.make_async_remote_copy(
        src_ref=src, dst_ref=dst, send_sem=send_sem, recv_sem=recv_sem, device_id=to, device_id_type=MESH
    )
    copy.start()
    return copy


def landed(dst, recv_sem, send_sem):
    pltpu.make_async_remote_copy(
        src_ref=dst, dst_ref=dst, send_sem=send_sem, recv_sem=recv_sem, device_id=moved(0, 0, 0, 1), device_id_type=MESH
    ).wait_recv()


def dot(a, b, ca, cb):
    return lax.dot_general(a, b, (((ca,), (cb,)), ((), ())), precision=highest, preferred_element_type=f32)


def sketch_kernel(
    x_ref, g_ref, m_ref, r_ref,
    moment_ref, s_out, gram_out,
    xall, gall, rt, acc, sp, pair, cs, rs, sall, gp, grs, gall2,
    own_sem, xs_sem, xa_sem, xb_sem, gs_sem, gr_sem, gd_sem, gk_sem,
    p_sem, zs_sem, zr_sem, as_sem, ar_sem, ak_sem, hs_sem, hr_sem, ts_sem, tr_sem,
):
    x, y, z, k = place()
    row = x * 4 + y
    ready = greet(
        [(a, b, 0, j) for a in range(4) for b in range(4) for j in range(2) if (a, b, j) != (0, 0, 0)]
        + [(0, 0, d, 0) for d in range(1, 16)]
    )
    own_x = pltpu.make_async_copy(x_ref, xall.at[row], own_sem.at[0])
    own_g = pltpu.make_async_copy(g_ref, gall.at[k, z], own_sem.at[1])
    own_x.start()
    own_g.start()
    rt[...] = r_ref[...].T
    own_x.wait()
    own_g.wait()
    ready()

    sent = []
    number = 0

    def half(which, owner):
        return xall.at[owner, pl.ds(64 * which, 64)]

    def pass_on(which, owner, along_x):
        nonlocal number
        sem = xb_sem if which else xa_sem
        for d in range(1, 4):
            to = moved(d, 0) if along_x else moved(0, d)
            sent.append(send(half(which, owner), half(which, owner), xs_sem.at[number], sem.at[owner], to))
            number += 1

    gnum = 0

    def pass_g(owner, ds):
        nonlocal gnum
        for d in ds:
            sent.append(
                send(gall.at[k, owner], gall.at[k, owner], gs_sem.at[gnum], gr_sem.at[owner], moved(0, 0, d))
            )
            gnum += 1

    pass_g(z, (4, 8, 12))
    pass_on(0, row, True)
    pass_on(1, row, False)
    pass_g(z, (1, 2, 15))
    pass_on(0, row, False)
    pass_on(1, row, True)
    for d in (1, 3, 2):
        ox = ((x + 4 - d) % 4) * 4 + y
        oy = x * 4 + (y + 4 - d) % 4
        landed(half(0, ox), xa_sem.at[ox], xs_sem.at[0])
        pass_on(0, ox, False)
        landed(half(1, oy), xb_sem.at[oy], xs_sem.at[0])
        pass_on(1, oy, True)
    for d in (4, 12, 8):
        oz = (z + 16 - d) % 16
        landed(gall.at[k, oz], gr_sem.at[oz], gs_sem.at[0])
        pass_g(oz, (1, 2, 15))
    for a in (0, 4, 8, 12):
        for d in (1, 2, 15):
            oz = (z + 16 - d + 16 - a) % 16
            landed(gall.at[k, oz], gr_sem.at[oz], gs_sem.at[0])
    sent.append(send(gall.at[k], gall.at[k], gd_sem.at[0], gk_sem.at[0], moved(0, 0, 0, 1)))
    landed(gall.at[1 - k], gk_sem.at[0], gd_sem.at[0])

    acc[...] = m_ref[...]
    waited = [(0, 0)]
    for dx in (0, 1, 3, 2):
        gx = (x + 4 - dx) % 4
        for dy in range(4):
            owner = gx * 4 + (y + 4 - dy) % 4
            if dy != 0:
                if dx != 0:
                    landed(half(0, owner), xa_sem.at[owner], xs_sem.at[0])
                    landed(half(1, owner), xb_sem.at[owner], xs_sem.at[0])
                else:
                    landed(half(0, owner), xa_sem.at[owner], xs_sem.at[0])
            elif dx != 0:
                landed(half(1, owner), xb_sem.at[owner], xs_sem.at[0])
        xs = xall[pl.ds(gx * 4, 4)].reshape(4, 2, 64, 800)
        total = None
        for j in range(2):
            gs = gall[j, pl.ds(gx * 4, 4)].reshape(256, 320)
            part = lax.dot_general(
                gs, xs[:, j].reshape(256, 800), (((0,), (0,)), ((), ())), preferred_element_type=f32
            )
            total = part if total is None else total + part
        acc[...] += total
    moment_ref[...] = acc[...]
    sp[...] = dot(rt[...], acc[...], 1, 1).reshape(2, 16, 8, 320)

    c = send(sp.at[1 - k], pair, p_sem.at[0], p_sem.at[1], moved(0, 0, 0, 1))
    c.wait()
    cs[...] = sp[k] + pair[...]
    copies = [
        send(cs.at[(z + d) % 16], rs.at[d], zs_sem.at[d], zr_sem.at[d], moved(0, 0, d)) for d in range(1, 16)
    ]
    total = cs[z]
    for d in range(1, 16):
        copies[d - 1].wait_recv()
        total = total + rs[d]
    sall[k, z] = total
    sent += copies
    for d in range(1, 16):
        sent.append(send(sall.at[k, z], sall.at[k, z], as_sem.at[d], ar_sem.at[z], moved(0, 0, d)))
    for d in range(1, 16):
        oz = (z + 16 - d) % 16
        landed(sall.at[k, oz], ar_sem.at[oz], as_sem.at[0])
    sent.append(send(sall.at[k], sall.at[k], ak_sem.at[0], ak_sem.at[1], moved(0, 0, 0, 1)))
    landed(sall.at[1 - k], ak_sem.at[1], ak_sem.at[0])

    s_all = sall[...].reshape(256, 320)
    s_out[...] = s_all
    gp[...] = dot(sall[k].reshape(128, 320), s_all, 1, 1).reshape(16, 8, 256)
    copies = []
    for i, (a, b) in enumerate(XY):
        to_row = ((x + a) % 4) * 4 + (y + b) % 4
        copies.append(send(gp.at[to_row], grs.at[i], hs_sem.at[i], hr_sem.at[i], moved(a, b)))
    total = gp[row]
    for i in range(15):
        copies[i].wait_recv()
        total = total + grs[i]
    gall2[k, row] = total
    sent += copies
    n = 0
    for j in range(2):
        for a, b in [(0, 0)] + XY:
            if (a, b, j) != (0, 0, 0):
                sent.append(
                    send(gall2.at[k, row], gall2.at[k, row], ts_sem.at[n], tr_sem.at[k, row], moved(a, b, 0, j))
                )
                n += 1
    for j in range(2):
        for a, b in [(0, 0)] + XY:
            if (a, b, j) != (0, 0, 0):
                owner = ((x + 4 - a) % 4) * 4 + (y + 4 - b) % 4
                kk = (k + j) % 2
                landed(gall2.at[kk, owner], tr_sem.at[kk, owner], ts_sem.at[0])
    gram_out[...] = gall2[...].reshape(256, 256)
    for c in sent:
        c.wait_send()


def wide(column):
    return jnp.broadcast_to(column, (8, 128))


def factor_64(tile, parity):
    sub = lax.broadcasted_iota(jnp.int32, (8, 128), 0)
    rows = [tile[8 * t : 8 * t + 8] for t in range(8)]
    for p in range(8):
        first = 64 * parity + 8 * p
        col = {t: [wide(rows[t][:, first + j : first + j + 1]) for j in range(8)] for t in range(p, 8)}
        pivots = jnp.ones((8, 128), f32)
        for j in range(8):
            b = {i: wide(col[p][j][i : i + 1]) for i in range(j, 8)}
            inverse = 1.0 / b[j]
            pivots = jnp.where(sub == j, b[j], pivots)
            line = wide(rows[p][j : j + 1])
            for t in range(p, 8):
                factor = col[t][j] * inverse
                if t == p:
                    factor = jnp.where(sub > j, factor, 0.0)
                for i in range(j + 1, 8):
                    col[t][i] = col[t][i] - factor * b[i]
                rows[t] = rows[t] - factor * line
        rows[p] = rows[p] * lax.rsqrt(pivots)
    return jnp.concatenate(rows, axis=0)


def basis_kernel(gram_ref, s_ref, moment_ref, bt_ref, right_ref, ah):
    ah[:, 0:256] = gram_ref[...]
    ah[:, 256:576] = s_ref[...]
    lane = lax.broadcasted_iota(jnp.int32, (64, 128), 1)
    line = lax.broadcasted_iota(jnp.int32, (64, 128), 0)
    for b in range(4):
        parity, low = b % 2, 64 * b
        own = (lane // 64) == parity
        unit = jnp.where(lane == line + 64 * (1 - parity), 1.0, 0.0)
        tile = jnp.where(own, ah[low : low + 64, 128 * (b // 2) : 128 * (b // 2) + 128], unit)
        inverse = jnp.where(own, 0.0, factor_64(tile, parity))
        first = 128 * ((b + 1) // 2)
        block = ah[low : low + 64, first:576]
        upper = dot(inverse, jnp.concatenate([block, block], axis=0), 1, 0)
        bt_ref[low : low + 64, :] = upper[:, 256 - first :]
        if b < 3:
            change = dot(upper[:, : 256 - first], upper, 0, 0)
            ah[low + 64 : 256, first:576] = ah[low + 64 : 256, first:576] - change[low + 64 - first :, :]
    right_ref[...] = dot(bt_ref[...], moment_ref[...], 1, 0).reshape(16, 16, 800)


def right_kernel(
    part_ref, right_out, squares_out,
    rs, rall, sq, sqs, sqall,
    s_sem, r_sem, as_sem, ar_sem, qs_sem, qr_sem, ts_sem, tr_sem,
):
    x, y, z, k = place()
    row = x * 4 + y
    cols = [(0, 0, d, j) for d in range(16) for j in range(2) if (d, j) != (0, 0)]
    ready = greet([(a, b, 0, 0) for a, b in XY] + cols)
    ready()
    sent = []
    copies = []
    for i, (a, b) in enumerate(XY):
        to_row = ((x + a) % 4) * 4 + (y + b) % 4
        copies.append(send(part_ref.at[to_row], rs.at[i], s_sem.at[i], r_sem.at[i], moved(a, b)))
    total = part_ref[row]
    for i in range(15):
        copies[i].wait_recv()
        total = total + rs[i]
    sent += copies
    rall[row] = total
    for i, (a, b) in enumerate(XY):
        sent.append(send(rall.at[row], rall.at[row], as_sem.at[i], ar_sem.at[row], moved(a, b)))
    sq[...] = jnp.broadcast_to(jnp.sum(total * total, axis=1, keepdims=True), (16, 128))
    copies = [send(sq, sqs.at[i], qs_sem.at[i], qr_sem.at[i], moved(*o)) for i, o in enumerate(cols)]
    total = sq[...]
    for i in range(31):
        copies[i].wait_recv()
        total = total + sqs[i]
    sent += copies
    sqall[row] = total
    for i, (a, b) in enumerate(XY):
        sent.append(send(sqall.at[row], sqall.at[row], ts_sem.at[i], tr_sem.at[row], moved(a, b)))
    for a, b in XY:
        owner = ((x + 4 - a) % 4) * 4 + (y + 4 - b) % 4
        landed(rall.at[owner], ar_sem.at[owner], as_sem.at[0])
    right_out[...] = rall[...].reshape(256, 800)
    for a, b in XY:
        owner = ((x + 4 - a) % 4) * 4 + (y + 4 - b) % 4
        landed(sqall.at[owner], tr_sem.at[owner], ts_sem.at[0])
    squares_out[...] = sqall[...].reshape(256, 128)
    for c in sent:
        c.wait_send()


def update_kernel(w_ref, moment_ref, bt_ref, right_ref, squares_ref, w_out, m_out, f_out):
    scale = lax.rsqrt(squares_ref[...][:, :1] / N + tiny_eps)
    basis = bt_ref[...].T
    right = right_ref[...]
    m_out[...] = moment_ref[...] - (1.0 - mix_rate) * dot(basis, right, 1, 0)
    factor = right * scale
    f_out[...] = factor.T
    w_out[...] = w_ref[...].astype(f32) * (1.0 - step_rate * weight_decay) - step_rate * math.sqrt(
        M / RANK
    ) * dot(basis, factor, 1, 0)


def vmem(count):
    return [pl.BlockSpec(memory_space=pltpu.VMEM)] * count


def shape(*dims):
    return jax.ShapeDtypeStruct(dims, f32)


def on_device(inputs, out_grads, weights, momentum, right_factor):
    dma = pltpu.SemaphoreType.DMA
    moment, sketch, gram = pl.pallas_call(
        sketch_kernel,
        name="sketch",
        out_shape=(shape(320, 800), shape(256, 320), shape(256, 256)),
        in_specs=vmem(4),
        out_specs=tuple(vmem(3)),
        scratch_shapes=[
            pltpu.VMEM((16, 128, 800), bf16),
            pltpu.VMEM((2, 16, 64, 320), bf16),
            pltpu.VMEM((256, 800), f32),
            pltpu.VMEM((320, 800), f32),
            pltpu.VMEM((2, 16, 8, 320), f32),
            pltpu.VMEM((16, 8, 320), f32),
            pltpu.VMEM((16, 8, 320), f32),
            pltpu.VMEM((16, 8, 320), f32),
            pltpu.VMEM((2, 16, 8, 320), f32),
            pltpu.VMEM((16, 8, 256), f32),
            pltpu.VMEM((15, 8, 256), f32),
            pltpu.VMEM((2, 16, 8, 256), f32),
            dma((2,)), dma((30,)), dma((16,)), dma((16,)), dma((15,)), dma((16,)), dma((1,)), dma((1,)),
            dma((2,)), dma((16,)), dma((16,)), dma((16,)), dma((16,)), dma((2,)), dma((15,)), dma((15,)),
            dma((31,)), dma((2, 16)),
        ],
        compiler_params=pltpu.CompilerParams(collective_id=0, has_side_effects=True, vmem_limit_bytes=VMEM_LIMIT),
    )(inputs, out_grads, momentum, right_factor)
    basis_t, part = pl.pallas_call(
        basis_kernel,
        name="basis",
        out_shape=(shape(256, 320), shape(16, 16, 800)),
        in_specs=vmem(3),
        out_specs=tuple(vmem(2)),
        scratch_shapes=[pltpu.VMEM((256, 576), f32)],
        compiler_params=pltpu.CompilerParams(vmem_limit_bytes=VMEM_LIMIT),
    )(gram, sketch, moment)
    right, squares = pl.pallas_call(
        right_kernel,
        name="right_side",
        out_shape=(shape(256, 800), shape(256, 128)),
        in_specs=vmem(1),
        out_specs=tuple(vmem(2)),
        scratch_shapes=[
            pltpu.VMEM((15, 16, 800), f32),
            pltpu.VMEM((16, 16, 800), f32),
            pltpu.VMEM((16, 128), f32),
            pltpu.VMEM((31, 16, 128), f32),
            pltpu.VMEM((16, 16, 128), f32),
            dma((15,)), dma((15,)), dma((15,)), dma((16,)), dma((31,)), dma((31,)), dma((15,)), dma((16,)),
        ],
        compiler_params=pltpu.CompilerParams(collective_id=1, has_side_effects=True, vmem_limit_bytes=VMEM_LIMIT),
    )(part)
    return tuple(
        pl.pallas_call(
            update_kernel,
            name="updates",
            out_shape=(shape(320, 800), shape(320, 800), shape(800, 256)),
            in_specs=vmem(5),
            out_specs=tuple(vmem(3)),
            compiler_params=pltpu.CompilerParams(vmem_limit_bytes=VMEM_LIMIT),
        )(weights, moment, basis_t, right, squares)
    )


def solution(mesh):
    return jax.shard_map(
        on_device,
        mesh=mesh,
        in_specs=(P("row", "col"), P("col", "row"), P("row", "col"), P("row", "col"), P("col", None)),
        out_specs=(P("row", "col"), P("row", "col"), P("col", None)),
        check_vma=False,
    )
```

time: 362 us -> 163 us (0.45)
  blocking collectives: 175 us -> 0 us
  Pallas kernels: 0 us -> 160 us
  waiting for transfers between devices: 75.9 us -> 0 us
  other arithmetic: 54.3 us -> 0 us
  matrix products: 16.7 us -> 0 us
  between operations: 15.6 us -> 0.65 us
  starting transfers between devices: 14.9 us -> 0 us
  local copies, waits for them, and re-layouts: 9.59 us -> 1.76 us
    pallas_call x0 -> x4, Pallas kernels: none -> 160 us  [the longest x1 94.5 us: on_device(): pl.pallas_call(sketch_kernel, name='sketch', out_shape=(shape(320, 800),...]
    all_to_all x5 -> x0, blocking collectives: 125 us -> none  [the longest x3 74.9 us: sum_at_owner(): pieces = lax.all_to_all(split_up(value, dim, peers), axis, 0, 0, tiled=True)]
    all_gather x2 -> x0, waiting for transfers between devices: 60.9 us -> none  [the longest x1 48.7 us: gathered_by_axis_2(): value = lax.all_gather(value, axis, axis=dim, tiled=True)]
    another operation x9 -> x0, other arithmetic: 53.9 us -> none  [the longest x6 33.9 us: orthonormal(): factor_low = jnp.linalg.cholesky(gram_total)]
    all_gather x2 -> x0, blocking collectives: 49.1 us -> none  [the longest x1 36.6 us: all_blocks(): pieces = lax.all_gather(pieces, axes[k])]
    dot_general x6 -> x0, matrix products: 15.4 us -> none  [the longest x1 4.23 us: on_device(): lax.dot_general(grads_all, gathered_by_axis_2(inputs, ROW, 0), (((0,), (0...]
    all_to_all x2 -> x0, waiting for transfers between devices: 14.9 us -> none  [from_everyone(): return lax.all_to_all(copies, axis, split_axis=0, concat_axis=0, tiled=True)]
    all_to_all x2 -> x0, starting transfers between devices: 14.8 us -> none  [from_everyone(): return lax.all_to_all(copies, axis, split_axis=0, concat_axis=0, tiled=True)]
  transfers between devices with their start and end apart: 4 -> 0, of which waited for: 4 -> 0; matrix products, arithmetic and copies ran while one was open for 2% -> 0% of each run, Pallas kernels for 0% -> 0%
where the time goes in v1:
time: 163 us; the launch traced here: 162 us
  Pallas kernels  160 us (98%)
  local copies, waits for them, and re-layouts  1.76 us (1%)
    pallas_call x1, Pallas kernels, on_device(): pl.pallas_call(sketch_kernel, name='sketch', out_shape=(shape(320, 800),...  94.5 us
    pallas_call x1, Pallas kernels, on_device(): pl.pallas_call(right_kernel, name='right_side', out_shape=(shape(256, 800...  46.7 us
    pallas_call x1, Pallas kernels, on_device(): pl.pallas_call(basis_kernel, name='basis', out_shape=(shape(256, 320), sh...  13.4 us
    pallas_call x1, Pallas kernels, on_device(): pl.pallas_call(update_kernel, name='updates', out_shape=(shape(320, 800),...  5.35 us

profile of v1, /device:TPU:1, one launch (start us, length us, event | category | flops | bytes accessed | tf_op | source)
XLA Modules:
  0.0 162.3 jit_solution(17355062410671479233)
XLA Ops:
  0.6 1.8 %copy.8.x_ref = bf16[128,800]{1,0:T(8,128)(2,1)} copy(bf16[128,800]{0,1:T(8,128)(2,1)} %param.5) | data formatting | bytes 409600 | tf_op args[0]
  2.4 94.5 %sketch.1 = (f32[320,800]{1,0:T(8,128)}, f32[256,320]{1,0:T(8,128)}, f32[256,256]{1,0:T(8,128)}) custom-call(bf16[128,800]{1,0:T(8,128)(2,1)} %copy.8.x_ref, bf16[64,320]{1,0:T(8,128)(2,1)} %g_ref.1, f32[320,800]{1,0:T(8,128)} %m_ref.1, f32[800,256]{1,0:T(8,128)} %r_ref.1), custom_call_target="tpu_custom_call" | custom-call | tf_op jit(solution)/shard_map/sketch/pallas_call | solution.py:331
  96.9 13.4 %basis.1 = (f32[256,320]{1,0:T(8,128)}, f32[16,16,800]{2,1,0:T(8,128)}) custom-call(f32[256,256]{1,0:T(8,128)} %get-tuple-element.11.gram_ref, f32[256,320]{1,0:T(8,128)} %get-tuple-element.12.s_ref, f32[320,800]{1,0:T(8,128)} %get-tuple-element.10.moment_ref), custom_call_target="tpu_custom_call" | custom-call | tf_op jit(solution)/shard_map/basis/pallas_call | solution.py:356
  110.3 46.7 %right_side.1 = (f32[256,800]{1,0:T(8,128)}, f32[256,128]{1,0:T(8,128)}) custom-call(f32[16,16,800]{2,1,0:T(8,128)} %get-tuple-element.14.part_ref), custom_call_target="tpu_custom_call" | custom-call | tf_op jit(solution)/shard_map/right_side/pallas_call | solution.py:365
  157.0 5.3 %updates.1 = (f32[320,800]{1,0:T(8,128)}, f32[320,800]{1,0:T(8,128)}, f32[800,256]{1,0:T(8,128)}) custom-call(bf16[320,800]{1,0:T(8,128)(2,1)} %w_ref.1, f32[320,800]{1,0:T(8,128)} %get-tuple-element.10.moment_ref, f32[256,320]{1,0:T(8,128)} %get-tuple-element.13.bt_ref, f32[256,800]{1,0:T(8,128)} %get-tuple-element.15.right_ref, ...), custom_call_target="tpu_custom_call" | custom-call | tf_op jit(solution)/shard_map/updates/pallas_call | solution.py:382

commit v2 on v1

--- a/solution.py
+++ b/solution.py
@@ -65,18 +65,21 @@
     return lax.dot_general(a, b, (((ca,), (cb,)), ((), ())), precision=highest, preferred_element_type=f32)
 
 
-def sketch_kernel(
+def step_kernel(
     x_ref, g_ref, m_ref, r_ref,
-    moment_ref, s_out, gram_out,
-    xall, gall, rt, acc, sp, pair, cs, rs, sall, gp, grs, gall2,
+    moment_ref, bt_ref, right_out, squares_out,
+    xall, gall, rt, acc, sp, pair, cs, rs, sall, gp, grs, gall2, ah,
+    part, brs, rall, sq, sq2, sqs, sqall,
     own_sem, xs_sem, xa_sem, xb_sem, gs_sem, gr_sem, gd_sem, gk_sem,
     p_sem, zs_sem, zr_sem, as_sem, ar_sem, ak_sem, hs_sem, hr_sem, ts_sem, tr_sem,
+    bs_sem, br_sem, cs_sem, cr_sem, qp_sem, qs_sem, qr_sem, us_sem, ur_sem,
 ):
     x, y, z, k = place()
     row = x * 4 + y
     ready = greet(
-        [(a, b, 0, j) for a in range(4) for b in range(4) for j in range(2) if (a, b, j) != (0, 0, 0)]
-        + [(0, 0, d, 0) for d in range(1, 16)]
+        [(0, 0, d, 0) for d in (8, 7, 9, 6, 10, 5, 11, 4, 12, 3, 13, 2, 14, 1, 15)]
+        + [(a, b, 0, 0) for a, b in XY[::-1]]
+        + [(0, 0, 0, 1)]
     )
     own_x = pltpu.make_async_copy(x_ref, xall.at[row], own_sem.at[0])
     own_g = pltpu.make_async_copy(g_ref, gall.at[k, z], own_sem.at[1])
@@ -153,10 +156,10 @@
         total = None
         for j in range(2):
             gs = gall[j, pl.ds(gx * 4, 4)].reshape(256, 320)
-            part = lax.dot_general(
+            piece = lax.dot_general(
                 gs, xs[:, j].reshape(256, 800), (((0,), (0,)), ((), ())), preferred_element_type=f32
             )
-            total = part if total is None else total + part
+            total = piece if total is None else total + piece
         acc[...] += total
     moment_ref[...] = acc[...]
     sp[...] = dot(rt[...], acc[...], 1, 1).reshape(2, 16, 8, 320)
@@ -182,8 +185,7 @@
     landed(sall.at[1 - k], ak_sem.at[1], ak_sem.at[0])
 
     s_all = sall[...].reshape(256, 320)
-    s_out[...] = s_all
-    gp[...] = dot(sall[k].reshape(128, 320), s_all, 1, 1).reshape(16, 8, 256)
+    gp[...] = dot(s_all, s_all, 1, 1).reshape(16, 16, 256)
     copies = []
     for i, (a, b) in enumerate(XY):
         to_row = ((x + a) % 4) * 4 + (y + b) % 4
@@ -192,23 +194,53 @@
     for i in range(15):
         copies[i].wait_recv()
         total = total + grs[i]
-    gall2[k, row] = total
+    gall2[row] = total
     sent += copies
-    n = 0
-    for j in range(2):
-        for a, b in [(0, 0)] + XY:
-            if (a, b, j) != (0, 0, 0):
-                sent.append(
-                    send(gall2.at[k, row], gall2.at[k, row], ts_sem.at[n], tr_sem.at[k, row], moved(a, b, 0, j))
-                )
-                n += 1
-    for j in range(2):
-        for a, b in [(0, 0)] + XY:
-            if (a, b, j) != (0, 0, 0):
-                owner = ((x + 4 - a) % 4) * 4 + (y + 4 - b) % 4
-                kk = (k + j) % 2
-                landed(gall2.at[kk, owner], tr_sem.at[kk, owner], ts_sem.at[0])
-    gram_out[...] = gall2[...].reshape(256, 256)
+    for i, (a, b) in enumerate(XY):
+        sent.append(send(gall2.at[row], gall2.at[row], ts_sem.at[i], tr_sem.at[row], moved(a, b)))
+    for a, b in XY:
+        owner = ((x + 4 - a) % 4) * 4 + (y + 4 - b) % 4
+        landed(gall2.at[owner], tr_sem.at[owner], ts_sem.at[0])
+
+    orthonormal(gall2[...].reshape(256, 256), s_all, bt_ref, ah)
+    part[...] = dot(bt_ref[...], acc[...], 1, 0).reshape(16, 16, 800)
+
+    copies = []
+    for i, (a, b) in enumerate(XY):
+        to_row = ((x + a) % 4) * 4 + (y + b) % 4
+        copies.append(send(part.at[to_row], brs.at[i], bs_sem.at[i], br_sem.at[i], moved(a, b)))
+    total = part[row]
+    for i in range(15):
+        copies[i].wait_recv()
+        total = total + brs[i]
+    sent += copies
+    rall[row] = total
+    diagonal = lax.broadcasted_iota(jnp.int32, (16, 128), 0) == lax.broadcasted_iota(jnp.int32, (16, 128), 1)
+    squares = jnp.sum(total * total, axis=1, keepdims=True)
+    sq[...] = jnp.sum(jnp.where(diagonal, squares, 0.0), axis=0, keepdims=True)
+    c = send(sq, sq2, qp_sem.at[0], qp_sem.at[1], moved(0, 0, 0, 1))
+    for i, (a, b) in enumerate(XY):
+        sent.append(send(rall.at[row], rall.at[row], cs_sem.at[i], cr_sem.at[row], moved(a, b)))
+    c.wait()
+    sq[...] = sq[...] + sq2[...]
+    copies = [send(sq, sqs.at[d], qs_sem.at[d], qr_sem.at[d], moved(0, 0, d)) for d in range(1, 16)]
+    total = sq[...]
+    for d in range(1, 16):
+        copies[d - 1].wait_recv()
+        total = total + sqs[d]
+    sent += copies
+    sqall[row] = total
+    for i, (a, b) in enumerate(XY):
+        sent.append(send(sqall.at[row], sqall.at[row], us_sem.at[i], ur_sem.at[row], moved(a, b)))
+    for a, b in XY:
+        owner = ((x + 4 - a) % 4) * 4 + (y + 4 - b) % 4
+        landed(rall.at[owner], cr_sem.at[owner], cs_sem.at[0])
+    right_out[...] = rall[...].reshape(256, 800)
+    for a, b in XY:
+        owner = ((x + 4 - a) % 4) * 4 + (y + 4 - b) % 4
+        landed(sqall.at[owner], ur_sem.at[owner], us_sem.at[0])
+    squares = jnp.sum(jnp.where(diagonal[None], sqall[...], 0.0), axis=2, keepdims=True)
+    squares_out[...] = jnp.broadcast_to(squares.reshape(256, 1), (256, 128))
     for c in sent:
         c.wait_send()
 
@@ -240,9 +272,9 @@
     return jnp.concatenate(rows, axis=0)
 
 
-def basis_kernel(gram_ref, s_ref, moment_ref, bt_ref, right_ref, ah):
-    ah[:, 0:256] = gram_ref[...]
-    ah[:, 256:576] = s_ref[...]
+def orthonormal(gram, sketch, bt_ref, ah):
+    ah[:, 0:256] = gram
+    ah[:, 256:576] = sketch
     lane = lax.broadcasted_iota(jnp.int32, (64, 128), 1)
     line = lax.broadcasted_iota(jnp.int32, (64, 128), 0)
     for b in range(4):
@@ -258,52 +290,6 @@
         if b < 3:
             change = dot(upper[:, : 256 - first], upper, 0, 0)
             ah[low + 64 : 256, first:576] = ah[low + 64 : 256, first:576] - change[low + 64 - first :, :]
-    right_ref[...] = dot(bt_ref[...], moment_ref[...], 1, 0).reshape(16, 16, 800)
-
-
-def right_kernel(
-    part_ref, right_out, squares_out,
-    rs, rall, sq, sqs, sqall,
-    s_sem, r_sem, as_sem, ar_sem, qs_sem, qr_sem, ts_sem, tr_sem,
-):
-    x, y, z, k = place()
-    row = x * 4 + y
-    cols = [(0, 0, d, j) for d in range(16) for j in range(2) if (d, j) != (0, 0)]
-    ready = greet([(a, b, 0, 0) for a, b in XY] + cols)
-    ready()
-    sent = []
-    copies = []
-    for i, (a, b) in enumerate(XY):
-        to_row = ((x + a) % 4) * 4 + (y + b) % 4
-        copies.append(send(part_ref.at[to_row], rs.at[i], s_sem.at[i], r_sem.at[i], moved(a, b)))
-    total = part_ref[row]
-    for i in range(15):
-        copies[i].wait_recv()
-        total = total + rs[i]
-    sent += copies
-    rall[row] = total
-    for i, (a, b) in enumerate(XY):
-        sent.append(send(rall.at[row], rall.at[row], as_sem.at[i], ar_sem.at[row], moved(a, b)))
-    sq[...] = jnp.broadcast_to(jnp.sum(total * total, axis=1, keepdims=True), (16, 128))
-    copies = [send(sq, sqs.at[i], qs_sem.at[i], qr_sem.at[i], moved(*o)) for i, o in enumerate(cols)]
-    total = sq[...]
-    for i in range(31):
-        copies[i].wait_recv()
-        total = total + sqs[i]
-    sent += copies
-    sqall[row] = total
-    for i, (a, b) in enumerate(XY):
-        sent.append(send(sqall.at[row], sqall.at[row], ts_sem.at[i], tr_sem.at[row], moved(a, b)))
-    for a, b in XY:
-        owner = ((x + 4 - a) % 4) * 4 + (y + 4 - b) % 4
-        landed(rall.at[owner], ar_sem.at[owner], as_sem.at[0])
-    right_out[...] = rall[...].reshape(256, 800)
-    for a, b in XY:
-        owner = ((x + 4 - a) % 4) * 4 + (y + 4 - b) % 4
-        landed(sqall.at[owner], tr_sem.at[owner], ts_sem.at[0])
-    squares_out[...] = sqall[...].reshape(256, 128)
-    for c in sent:
-        c.wait_send()
 
 
 def update_kernel(w_ref, moment_ref, bt_ref, right_ref, squares_ref, w_out, m_out, f_out):
@@ -328,12 +314,12 @@
 
 def on_device(inputs, out_grads, weights, momentum, right_factor):
     dma = pltpu.SemaphoreType.DMA
-    moment, sketch, gram = pl.pallas_call(
-        sketch_kernel,
-        name="sketch",
-        out_shape=(shape(320, 800), shape(256, 320), shape(256, 256)),
+    moment, basis_t, right, squares = pl.pallas_call(
+        step_kernel,
+        name="step",
+        out_shape=(shape(320, 800), shape(256, 320), shape(256, 800), shape(256, 128)),
         in_specs=vmem(4),
-        out_specs=tuple(vmem(3)),
+        out_specs=tuple(vmem(4)),
         scratch_shapes=[
             pltpu.VMEM((16, 128, 800), bf16),
             pltpu.VMEM((2, 16, 64, 320), bf16),
@@ -344,40 +330,24 @@
             pltpu.VMEM((16, 8, 320), f32),
             pltpu.VMEM((16, 8, 320), f32),
             pltpu.VMEM((2, 16, 8, 320), f32),
-            pltpu.VMEM((16, 8, 256), f32),
-            pltpu.VMEM((15, 8, 256), f32),
-            pltpu.VMEM((2, 16, 8, 256), f32),
+            pltpu.VMEM((16, 16, 256), f32),
+            pltpu.VMEM((15, 16, 256), f32),
+            pltpu.VMEM((16, 16, 256), f32),
+            pltpu.VMEM((256, 576), f32),
+            pltpu.VMEM((16, 16, 800), f32),
+            pltpu.VMEM((15, 16, 800), f32),
+            pltpu.VMEM((16, 16, 800), f32),
+            pltpu.VMEM((1, 128), f32),
+            pltpu.VMEM((1, 128), f32),
+            pltpu.VMEM((16, 1, 128), f32),
+            pltpu.VMEM((16, 1, 128), f32),
             dma((2,)), dma((30,)), dma((16,)), dma((16,)), dma((15,)), dma((16,)), dma((1,)), dma((1,)),
             dma((2,)), dma((16,)), dma((16,)), dma((16,)), dma((16,)), dma((2,)), dma((15,)), dma((15,)),
-            dma((31,)), dma((2, 16)),
+            dma((15,)), dma((16,)),
+            dma((15,)), dma((15,)), dma((15,)), dma((16,)), dma((2,)), dma((16,)), dma((16,)), dma((15,)), dma((16,)),
         ],
         compiler_params=pltpu.CompilerParams(collective_id=0, has_side_effects=True, vmem_limit_bytes=VMEM_LIMIT),
     )(inputs, out_grads, momentum, right_factor)
-    basis_t, part = pl.pallas_call(
-        basis_kernel,
-        name="basis",
-        out_shape=(shape(256, 320), shape(16, 16, 800)),
-        in_specs=vmem(3),
-        out_specs=tuple(vmem(2)),
-        scratch_shapes=[pltpu.VMEM((256, 576), f32)],
-        compiler_params=pltpu.CompilerParams(vmem_limit_bytes=VMEM_LIMIT),
-    )(gram, sketch, moment)
-    right, squares = pl.pallas_call(
-        right_kernel,
-        name="right_side",
-        out_shape=(shape(256, 800), shape(256, 128)),
-        in_specs=vmem(1),
-        out_specs=tuple(vmem(2)),
-        scratch_shapes=[
-            pltpu.VMEM((15, 16, 800), f32),
-            pltpu.VMEM((16, 16, 800), f32),
-            pltpu.VMEM((16, 128), f32),
-            pltpu.VMEM((31, 16, 128), f32),
-            pltpu.VMEM((16, 16, 128), f32),
-            dma((15,)), dma((15,)), dma((15,)), dma((16,)), dma((31,)), dma((31,)), dma((15,)), dma((16,)),
-        ],
-        compiler_params=pltpu.CompilerParams(collective_id=1, has_side_effects=True, vmem_limit_bytes=VMEM_LIMIT),
-    )(part)
     return tuple(
         pl.pallas_call(
             update_kernel,

time: 163 us -> 142 us (0.87)
  Pallas kernels: 160 us -> 139 us
    pallas_call x3 -> x1, Pallas kernels: 155 us -> 134 us  [on_device(): pl.pallas_call(step_kernel, name='step', out_shape=(shape(320, 800), shap...]
where the time goes in v2:
time: 142 us; the launch traced here: 141 us
  Pallas kernels  139 us (98%)
  local copies, waits for them, and re-layouts  1.76 us (1%)
    pallas_call x1, Pallas kernels, on_device(): pl.pallas_call(step_kernel, name='step', out_shape=(shape(320, 800), shap...  134 us
    pallas_call x1, Pallas kernels, on_device(): pl.pallas_call(update_kernel, name='updates', out_shape=(shape(320, 800),...  5.35 us

profile of v2, /device:TPU:1, one launch (start us, length us, event | category | flops | bytes accessed | tf_op | source)
XLA Modules:
  0.0 141.3 jit_solution(13873675259272772519)
XLA Ops:
  0.6 1.8 %copy.8.x_ref = bf16[128,800]{1,0:T(8,128)(2,1)} copy(bf16[128,800]{0,1:T(8,128)(2,1)} %param.5) | data formatting | bytes 409600 | tf_op args[0]
  2.4 133.5 %step.1 = (f32[320,800]{1,0:T(8,128)}, f32[256,320]{1,0:T(8,128)}, f32[256,800]{1,0:T(8,128)}, f32[256,128]{1,0:T(8,128)}) custom-call(bf16[128,800]{1,0:T(8,128)(2,1)} %copy.8.x_ref, bf16[64,320]{1,0:T(8,128)(2,1)} %g_ref.1, f32[320,800]{1,0:T(8,128)} %m_ref.1, f32[800,256]{1,0:T(8,128)} %r_ref.1), custom_call_target="tpu_custom_call" | custom-call | tf_op jit(solution)/shard_map/step/pallas_call | solution.py:317
  135.9 5.4 %updates.1 = (f32[320,800]{1,0:T(8,128)}, f32[320,800]{1,0:T(8,128)}, f32[800,256]{1,0:T(8,128)}) custom-call(bf16[320,800]{1,0:T(8,128)(2,1)} %w_ref.1, f32[320,800]{1,0:T(8,128)} %get-tuple-element.7.moment_ref, f32[256,320]{1,0:T(8,128)} %get-tuple-element.8.bt_ref, f32[256,800]{1,0:T(8,128)} %get-tuple-element.9.right_ref, ...), custom_call_target="tpu_custom_call" | custom-call | tf_op jit(solution)/shard_map/updates/pallas_call | solution.py:352

commit v3 on v2

v3 whole, which is shorter than its diff:
```python
import functools
import math

import jax
import jax.numpy as jnp
from jax import lax
from jax.experimental import pallas as pl
from jax.experimental.pallas import tpu as pltpu
from jax.sharding import PartitionSpec as P

M = 5120
N = 25600
RANK = 256
TOKENS = 2048

mix_rate = 0.95
step_rate = 0.3
weight_decay = 0.1
tiny_eps = 1e-06
highest = lax.Precision.HIGHEST
MESH = pl.DeviceIdType.MESH
f32 = jnp.float32
bf16 = jnp.bfloat16
VMEM_LIMIT = 56 * 2**20
XY = [(a, b) for a in range(4) for b in range(4) if (a, b) != (0, 0)]


def place():
    r = lax.axis_index("row")
    c = lax.axis_index("col")
    return r // 4, r % 4, c // 2, c % 2


def at(x, y, z, k):
    return (x * 4 + y, z * 2 + k)


def moved(dx=0, dy=0, dz=0, dk=0):
    x, y, z, k = place()
    return at((x + dx) % 4, (y + dy) % 4, (z + dz) % 16, (k + dk) % 2)


def greet(offsets):
    barrier = pltpu.get_barrier_semaphore()
    for o in offsets:
        pl.semaphore_signal(barrier, inc=1, device_id=moved(*o), device_id_type=MESH)
    return lambda: pl.semaphore_wait(barrier, len(offsets))


def send(src, dst, send_sem, recv_sem, to):
    copy = pltpu.make_async_remote_copy(
        src_ref=src, dst_ref=dst, send_sem=send_sem, recv_sem=recv_sem, device_id=to, device_id_type=MESH
    )
    copy.start()
    return copy


def landed(dst, recv_sem, send_sem):
    pltpu.make_async_remote_copy(
        src_ref=dst, dst_ref=dst, send_sem=send_sem, recv_sem=recv_sem, device_id=moved(0, 0, 0, 1), device_id_type=MESH
    ).wait_recv()


def dot(a, b, ca, cb):
    return lax.dot_general(a, b, (((ca,), (cb,)), ((), ())), precision=highest, preferred_element_type=f32)


def dot_bf16(a, b, ca, cb):
    return lax.dot_general(a, b, (((ca,), (cb,)), ((), ())), preferred_element_type=f32)


NEAR_Z = (1, 15, 2, 14, 3, 13, 4, 12, 5, 11, 6, 10, 7, 9, 8)


def halves(value):
    high = value.astype(bf16)
    return high, (value - high.astype(f32)).astype(bf16)


BALANCED = [(1, 0), (0, 1), (3, 0), (0, 3), (1, 1), (3, 3), (1, 3), (3, 1), (2, 0), (0, 2), (1, 2), (2, 1), (3, 2), (2, 3), (2, 2)]


def step_kernel(
    x_ref, g_ref, m_ref, r_ref,
    moment_ref, high_ref, low_ref, right_out, squares_out,
    xall, gall, rt, acc, sp, pair, cs, rs, sall, gp, grs, gall2, ah, bt,
    part, brs, rall, sq, sq2, sqs, sqall,
    own_sem, xs_sem, xa_sem, xb_sem, gs_sem, gr_sem, gd_sem, gk_sem,
    p_sem, zs_sem, zr_sem, as_sem, ar_sem, aks_sem, akr_sem, hs_sem, hr_sem, ts_sem, tr_sem,
    bs_sem, br_sem, cs_sem, cr_sem, qp_sem, qs_sem, qr_sem, us_sem, ur_sem,
):
    x, y, z, k = place()
    row = x * 4 + y
    ready = greet(
        [(0, 0, d, 0) for d in NEAR_Z[::-1]]
        + [(a, b, 0, 0) for a, b in XY[::-1]]
        + [(0, 0, 0, 1)]
    )
    own_x = pltpu.make_async_copy(x_ref, xall.at[row], own_sem.at[0])
    own_g = pltpu.make_async_copy(g_ref, gall.at[z, k], own_sem.at[1])
    own_x.start()
    own_g.start()
    rt[...] = r_ref[...].T
    own_x.wait()
    own_g.wait()
    ready()

    sent = []
    number = 0
    gnum = 0

    def half(which, owner):
        return xall.at[owner, pl.ds(400 * which, 400)]

    def pass_on(which, owner, along_x, ds):
        nonlocal number
        sem = xb_sem if which else xa_sem
        for d in ds:
            to = moved(d, 0) if along_x else moved(0, d)
            sent.append(send(half(which, owner), half(which, owner), xs_sem.at[number], sem.at[owner], to))
            number += 1

    def pass_g(owner, ds):
        nonlocal gnum
        for d in ds:
            sent.append(
                send(gall.at[owner, k], gall.at[owner, k], gs_sem.at[gnum], gr_sem.at[owner], moved(0, 0, d))
            )
            gnum += 1

    def cross_g(owner):
        sent.append(send(gall.at[owner, k], gall.at[owner, k], gd_sem.at[owner], gk_sem.at[owner], moved(0, 0, 0, 1)))

    pass_g(z, (8, 4, 12))
    for d in (1, 3, 2):
        pass_on(0, row, True, (d,))
        pass_on(1, row, False, (d,))
    pass_g(z, (1, 15, 2))
    cross_g(z)
    for d in (1, 3, 2):
        pass_on(0, row, False, (d,))
        pass_on(1, row, True, (d,))
    for d in (1, 3, 2):
        ox = ((x + 4 - d) % 4) * 4 + y
        oy = x * 4 + (y + 4 - d) % 4
        landed(half(0, ox), xa_sem.at[ox], xs_sem.at[0])
        landed(half(1, oy), xb_sem.at[oy], xs_sem.at[0])
        for e in (1, 3, 2):
            pass_on(0, ox, False, (e,))
            pass_on(1, oy, True, (e,))
    for d in (4, 12, 8):
        oz = (z + 16 - d) % 16
        landed(gall.at[oz, k], gr_sem.at[oz], gs_sem.at[0])
        pass_g(oz, (1, 15, 2))
        cross_g(oz)
    for a in (0, 4, 12, 8):
        for d in (1, 15, 2):
            oz = (z + 32 - d - a) % 16
            landed(gall.at[oz, k], gr_sem.at[oz], gs_sem.at[0])
            cross_g(oz)
    for i in range(16):
        landed(gall.at[i, 1 - k], gk_sem.at[i], gd_sem.at[0])
    for a, b in XY:
        owner = ((x + 4 - a) % 4) * 4 + (y + 4 - b) % 4
        if b != 0:
            landed(half(0, owner), xa_sem.at[owner], xs_sem.at[0])
        if a != 0:
            landed(half(1, owner), xb_sem.at[owner], xs_sem.at[0])

    columns = jnp.concatenate([xall[i] for i in range(16)], axis=1)
    acc[...] = m_ref[...] + dot_bf16(gall[...].reshape(2048, 320), columns, 0, 1)
    sp[...] = dot(rt[...], acc[...], 1, 1).reshape(2, 16, 8, 320)

    c = send(sp.at[1 - k], pair, p_sem.at[0], p_sem.at[1], moved(0, 0, 0, 1))
    moment_ref[...] = acc[...]
    c.wait()
    cs[...] = sp[k] + pair[...]
    copies = [
        send(cs.at[(z + d) % 16], rs.at[d], zs_sem.at[d], zr_sem.at[d], moved(0, 0, d)) for d in NEAR_Z[::-1]
    ]
    total = cs[z]
    for i in range(15):
        copies[14 - i].wait_recv()
        total = total + rs[NEAR_Z[i]]
    sent += copies
    sall[k, z] = total
    for d in NEAR_Z[::-1]:
        sent.append(send(sall.at[k, z], sall.at[k, z], as_sem.at[d], ar_sem.at[z], moved(0, 0, d)))
    sent.append(send(sall.at[k, z], sall.at[k, z], aks_sem.at[z], akr_sem.at[z], moved(0, 0, 0, 1)))
    for d in NEAR_Z:
        oz = (z + 16 - d) % 16
        landed(sall.at[k, oz], ar_sem.at[oz], as_sem.at[0])
        sent.append(send(sall.at[k, oz], sall.at[k, oz], aks_sem.at[oz], akr_sem.at[oz], moved(0, 0, 0, 1)))
    for i in range(16):
        landed(sall.at[1 - k, i], akr_sem.at[i], aks_sem.at[0])

    s_all = sall[...].reshape(256, 320)
    gp[...] = dot(s_all, s_all, 1, 1).reshape(16, 16, 256)
    copies = []
    for i, (a, b) in enumerate(XY):
        to_row = ((x + a) % 4) * 4 + (y + b) % 4
        copies.append(send(gp.at[to_row], grs.at[i], hs_sem.at[i], hr_sem.at[i], moved(a, b)))
    total = gp[row]
    for i in range(15):
        copies[i].wait_recv()
        total = total + grs[i]
    gall2[row] = total
    sent += copies
    for i, (a, b) in enumerate(XY):
        sent.append(send(gall2.at[row], gall2.at[row], ts_sem.at[i], tr_sem.at[row], moved(a, b)))
    for a, b in XY:
        owner = ((x + 4 - a) % 4) * 4 + (y + 4 - b) % 4
        landed(gall2.at[owner], tr_sem.at[owner], ts_sem.at[0])

    ah[:, 0:256] = gall2[...].reshape(256, 256)
    ah[:, 256:576] = s_all
    right_copies = []
    for h in range(2):
        orthonormal((2 * h, 2 * h + 1), bt, ah)
        part[h] = dot(bt[128 * h : 128 * h + 128, :], acc[...], 1, 0).reshape(16, 8, 800)
        right_copies.append([])
        for i, (a, b) in enumerate(BALANCED):
            to_row = ((x + a) % 4) * 4 + (y + b) % 4
            right_copies[h].append(
                send(part.at[h, to_row], brs.at[h, i], bs_sem.at[h, i], br_sem.at[h, i], moved(a, b))
            )
    sums = []
    for h in range(2):
        total = part[h, row]
        for i in range(15):
            right_copies[h][i].wait_recv()
            total = total + brs[h, i]
        sent += right_copies[h]
        rall[h, row] = total
        sums.append(jnp.sum(total * total, axis=1, keepdims=True))
        if h == 1:
            diagonal = lax.broadcasted_iota(jnp.int32, (16, 128), 0) == lax.broadcasted_iota(jnp.int32, (16, 128), 1)
            squares = jnp.concatenate(sums, axis=0)
            sq[...] = jnp.sum(jnp.where(diagonal, squares, 0.0), axis=0, keepdims=True)
            c = send(sq, sq2, qp_sem.at[0], qp_sem.at[1], moved(0, 0, 0, 1))
        for i, (a, b) in enumerate(BALANCED):
            sent.append(send(rall.at[h, row], rall.at[h, row], cs_sem.at[h, i], cr_sem.at[h, row], moved(a, b)))
    c.wait()
    sq[...] = sq[...] + sq2[...]
    copies = [send(sq, sqs.at[d], qs_sem.at[d], qr_sem.at[d], moved(0, 0, d)) for d in NEAR_Z[::-1]]
    high_ref[...], low_ref[...] = halves(bt[...].T)
    total = sq[...]
    for i in range(15):
        copies[14 - i].wait_recv()
        total = total + sqs[NEAR_Z[i]]
    sent += copies
    sqall[row] = total
    for i, (a, b) in enumerate(BALANCED):
        sent.append(send(sqall.at[row], sqall.at[row], us_sem.at[i], ur_sem.at[row], moved(a, b)))
    for h in range(2):
        for a, b in XY:
            owner = ((x + 4 - a) % 4) * 4 + (y + 4 - b) % 4
            landed(rall.at[h, owner], cr_sem.at[h, owner], cs_sem.at[0, 0])
        right_out[128 * h : 128 * h + 128, :] = rall[h].reshape(128, 800)
    for a, b in XY:
        owner = ((x + 4 - a) % 4) * 4 + (y + 4 - b) % 4
        landed(sqall.at[owner], ur_sem.at[owner], us_sem.at[0])
    lane = lax.broadcasted_iota(jnp.int32, (16, 8, 128), 2)
    line = lax.broadcasted_iota(jnp.int32, (16, 8, 128), 1)
    rows = jnp.broadcast_to(sqall[...], (16, 8, 128))
    for h in range(2):
        squares = jnp.sum(jnp.where(lane == line + 8 * h, rows, 0.0), axis=2, keepdims=True)
        squares_out[128 * h : 128 * h + 128, :] = jnp.broadcast_to(squares.reshape(128, 1), (128, 128))
    for c in sent:
        c.wait_send()


def wide(column):
    return jnp.broadcast_to(column, (8, 128))


def factor_64(tile, parity):
    sub = lax.broadcasted_iota(jnp.int32, (8, 128), 0)
    rows = [tile[8 * t : 8 * t + 8] for t in range(8)]
    for p in range(8):
        first = 64 * parity + 8 * p
        col = {t: [wide(rows[t][:, first + j : first + j + 1]) for j in range(8)] for t in range(p, 8)}
        pivots = jnp.ones((8, 128), f32)
        for j in range(8):
            b = {i: wide(col[p][j][i : i + 1]) for i in range(j, 8)}
            inverse = 1.0 / b[j]
            pivots = jnp.where(sub == j, b[j], pivots)
            line = wide(rows[p][j : j + 1])
            for t in range(p, 8):
                factor = col[t][j] * inverse
                if t == p:
                    factor = jnp.where(sub > j, factor, 0.0)
                for i in range(j + 1, 8):
                    col[t][i] = col[t][i] - factor * b[i]
                rows[t] = rows[t] - factor * line
        rows[p] = rows[p] * lax.rsqrt(pivots)
    return jnp.concatenate(rows, axis=0)


def orthonormal(blocks, bt_ref, ah):
    lane = lax.broadcasted_iota(jnp.int32, (64, 128), 1)
    line = lax.broadcasted_iota(jnp.int32, (64, 128), 0)
    for b in blocks:
        parity, low = b % 2, 64 * b
        own = (lane // 64) == parity
        unit = jnp.where(lane == line + 64 * (1 - parity), 1.0, 0.0)
        tile = jnp.where(own, ah[low : low + 64, 128 * (b // 2) : 128 * (b // 2) + 128], unit)
        inverse = jnp.where(own, 0.0, factor_64(tile, parity))
        first = 128 * ((b + 1) // 2)
        block = ah[low : low + 64, first:576]
        upper = dot(inverse, jnp.concatenate([block, block], axis=0), 1, 0)
        bt_ref[low : low + 64, :] = upper[:, 256 - first :]
        if b < 3:
            change = dot(upper[:, : 256 - first], upper, 0, 0)
            ah[low + 64 : 256, first:576] = ah[low + 64 : 256, first:576] - change[low + 64 - first :, :]


def update_kernel(w_ref, moment_ref, high_ref, low_ref, right_ref, squares_ref, w_out, m_out, f_out, terms):
    @pl.when(pl.program_id(0) == 0)
    def _():
        right = right_ref[...]
        factor = right * lax.rsqrt(squares_ref[...][:, :1] / N + tiny_eps)
        f_out[...] = factor.T
        terms[0], terms[1] = halves(right)
        terms[2], terms[3] = halves(factor)

    high, low = high_ref[...], low_ref[...]

    def product(first, second):
        rest = dot_bf16(high, terms[second], 1, 0) + dot_bf16(low, terms[first], 1, 0)
        return dot_bf16(high, terms[first], 1, 0) + rest

    m_out[...] = moment_ref[...] - (1.0 - mix_rate) * product(0, 1)
    w_out[...] = w_ref[...].astype(f32) * (1.0 - step_rate * weight_decay) - step_rate * math.sqrt(
        M / RANK
    ) * product(2, 3)


def vmem(count):
    return [pl.BlockSpec(memory_space=pltpu.VMEM)] * count


def shape(*dims):
    return jax.ShapeDtypeStruct(dims, f32)


def on_device(inputs, out_grads, weights, momentum, right_factor):
    dma = pltpu.SemaphoreType.DMA
    moment, high, low, right, squares = pl.pallas_call(
        step_kernel,
        name="step",
        out_shape=(
            shape(320, 800),
            jax.ShapeDtypeStruct((320, 256), bf16),
            jax.ShapeDtypeStruct((320, 256), bf16),
            shape(256, 800),
            shape(256, 128),
        ),
        in_specs=vmem(4),
        out_specs=tuple(vmem(5)),
        scratch_shapes=[
            pltpu.VMEM((16, 800, 128), bf16),
            pltpu.VMEM((16, 2, 64, 320), bf16),
            pltpu.VMEM((256, 800), f32),
            pltpu.VMEM((320, 800), f32),
            pltpu.VMEM((2, 16, 8, 320), f32),
            pltpu.VMEM((16, 8, 320), f32),
            pltpu.VMEM((16, 8, 320), f32),
            pltpu.VMEM((16, 8, 320), f32),
            pltpu.VMEM((2, 16, 8, 320), f32),
            pltpu.VMEM((16, 16, 256), f32),
            pltpu.VMEM((15, 16, 256), f32),
            pltpu.VMEM((16, 16, 256), f32),
            pltpu.VMEM((256, 576), f32),
            pltpu.VMEM((256, 320), f32),
            pltpu.VMEM((2, 16, 8, 800), f32),
            pltpu.VMEM((2, 15, 8, 800), f32),
            pltpu.VMEM((2, 16, 8, 800), f32),
            pltpu.VMEM((1, 128), f32),
            pltpu.VMEM((1, 128), f32),
            pltpu.VMEM((16, 1, 128), f32),
            pltpu.VMEM((16, 1, 128), f32),
            dma((2,)), dma((30,)), dma((16,)), dma((16,)), dma((18,)), dma((16,)), dma((16,)), dma((16,)),
            dma((2,)), dma((16,)), dma((16,)), dma((16,)), dma((16,)), dma((16,)), dma((16,)),
            dma((15,)), dma((15,)), dma((15,)), dma((16,)),
            dma((2, 15)), dma((2, 15)), dma((2, 15)), dma((2, 16)),
            dma((2,)), dma((16,)), dma((16,)), dma((15,)), dma((16,)),
        ],
        compiler_params=pltpu.CompilerParams(collective_id=0, has_side_effects=True, vmem_limit_bytes=VMEM_LIMIT),
    )(inputs.T, out_grads, momentum, right_factor)
    lines, whole = (lambda i: (i, 0)), (lambda i: (0, 0))
    return tuple(
        pl.pallas_call(
            update_kernel,
            name="updates",
            grid=(4,),
            out_shape=(shape(320, 800), shape(320, 800), shape(800, 256)),
            in_specs=[
                pl.BlockSpec((80, 800), lines),
                pl.BlockSpec((80, 800), lines),
                pl.BlockSpec((80, 256), lines),
                pl.BlockSpec((80, 256), lines),
                pl.BlockSpec((256, 800), whole),
                pl.BlockSpec((256, 128), whole),
            ],
            out_specs=(
                pl.BlockSpec((80, 800), lines),
                pl.BlockSpec((80, 800), lines),
                pl.BlockSpec((800, 256), whole),
            ),
            scratch_shapes=[pltpu.VMEM((4, 256, 800), bf16)],
            compiler_params=pltpu.CompilerParams(vmem_limit_bytes=VMEM_LIMIT),
        )(weights, moment, high, low, right, squares)
    )


def solution(mesh):
    return jax.shard_map(
        on_device,
        mesh=mesh,
        in_specs=(P("row", "col"), P("col", "row"), P("row", "col"), P("row", "col"), P("col", None)),
        out_specs=(P("row", "col"), P("row", "col"), P("col", None)),
        check_vma=False,
    )
```

time: 142 us -> 130 us (0.915)
  Pallas kernels: 139 us -> 129 us
  local copies, waits for them, and re-layouts: 1.76 us -> 0 us
    pallas_call x2, Pallas kernels: 139 us -> 129 us  [the longest x1 123 us: on_device(): pl.pallas_call(step_kernel, name='step', out_shape=(shape(320, 800), jax....]
    unnamed x1 -> x0, local copies, waits for them, and re-layouts: 1.76 us -> none
where the time goes in v3:
time: 130 us; the launch traced here: 129 us
  Pallas kernels  129 us (99%)
    pallas_call x1, Pallas kernels, on_device(): pl.pallas_call(step_kernel, name='step', out_shape=(shape(320, 800), jax....  123 us
    pallas_call x1, Pallas kernels, on_device(): pl.pallas_call(update_kernel, name='updates', grid=(4,), out_shape=(shape...  5.77 us

profile of v3, /device:TPU:1, one launch (start us, length us, event | category | flops | bytes accessed | tf_op | source)
XLA Modules:
  0.0 129.3 jit_solution(711894795664040507)
XLA Ops:
  0.6 122.8 %step.1 = (f32[320,800]{1,0:T(8,128)}, bf16[320,256]{1,0:T(8,128)(2,1)}, bf16[320,256]{1,0:T(8,128)(2,1)}, f32[256,800]{1,0:T(8,128)}, f32[256,128]{1,0:T(8,128)}) custom-call(bf16[800,128]{1,0:T(8,128)(2,1)} %bitcast.1, bf16[64,320]{1,0:T(8,128)(2,1)} %g_ref.1, f32[320,800]{1,0:T(8,128)} %m_ref.1, f32[800,256]{1,0:T(8,128)} %r_ref.1), custom_call_target="tpu_custom_call" | custom-call | tf_op jit(solution)/shard_map/step/pallas_call | solution.py:349
  123.4 5.8 %updates.1 = (f32[320,800]{1,0:T(8,128)}, f32[320,800]{1,0:T(8,128)}, f32[800,256]{1,0:T(8,128)}) custom-call(bf16[320,800]{1,0:T(8,128)(2,1)} %w_ref.1, f32[320,800]{1,0:T(8,128)} %get-tuple-element.8.moment_ref, bf16[320,256]{1,0:T(8,128)(2,1)} %get-tuple-element.9.high_ref, bf16[320,256]{1,0:T(8,128)(2,1)} %get-tuple-element.10.low_ref, ...), custom_call_target="tpu_custom_call" | custom-call | tf_op jit(solution)/shard_map/updates/pallas_call | solution.py:393

commit v4 on v3

--- a/solution.py
+++ b/solution.py
@@ -82,12 +82,12 @@
 
 def step_kernel(
     x_ref, g_ref, m_ref, r_ref,
-    moment_ref, high_ref, low_ref, right_out, squares_out,
-    xall, gall, rt, acc, sp, pair, cs, rs, sall, gp, grs, gall2, ah, bt,
-    part, brs, rall, sq, sq2, sqs, sqall,
+    moment_ref, basis_out, high_ref, low_ref, right_out, squares_out,
+    xall, gall, rt, acc, sp, pair, cs, rs, sall, gp, grs, gall2, ah,
+    part, brs, rall, sq, sq2, sqs,
     own_sem, xs_sem, xa_sem, xb_sem, gs_sem, gr_sem, gd_sem, gk_sem,
     p_sem, zs_sem, zr_sem, as_sem, ar_sem, aks_sem, akr_sem, hs_sem, hr_sem, ts_sem, tr_sem,
-    bs_sem, br_sem, cs_sem, cr_sem, qp_sem, qs_sem, qr_sem, us_sem, ur_sem,
+    bs_sem, br_sem, cs_sem, cr_sem, qp_sem, qs_sem, qr_sem,
 ):
     x, y, z, k = place()
     row = x * 4 + y
@@ -98,8 +98,10 @@
     )
     own_x = pltpu.make_async_copy(x_ref, xall.at[row], own_sem.at[0])
     own_g = pltpu.make_async_copy(g_ref, gall.at[z, k], own_sem.at[1])
+    own_m = pltpu.make_async_copy(m_ref, acc, own_sem.at[2])
     own_x.start()
     own_g.start()
+    own_m.start()
     rt[...] = r_ref[...].T
     own_x.wait()
     own_g.wait()
@@ -168,11 +170,16 @@
             landed(half(1, owner), xb_sem.at[owner], xs_sem.at[0])
 
     columns = jnp.concatenate([xall[i] for i in range(16)], axis=1)
-    acc[...] = m_ref[...] + dot_bf16(gall[...].reshape(2048, 320), columns, 0, 1)
-    sp[...] = dot(rt[...], acc[...], 1, 1).reshape(2, 16, 8, 320)
+    own_m.wait()
+    acc[...] += dot_bf16(gall[...].reshape(2048, 320), columns, 0, 1)
+    moment_copy = pltpu.make_async_copy(acc, moment_ref, own_sem.at[3])
+    moment_copy.start()
+    other = rt[pl.ds(pl.multiple_of(128 * (1 - k), 128), 128), :]
+    sp[1 - k] = dot(other, acc[...], 1, 1).reshape(16, 8, 320)
 
     c = send(sp.at[1 - k], pair, p_sem.at[0], p_sem.at[1], moved(0, 0, 0, 1))
-    moment_ref[...] = acc[...]
+    own = rt[pl.ds(pl.multiple_of(128 * k, 128), 128), :]
+    sp[k] = dot(own, acc[...], 1, 1).reshape(16, 8, 320)
     c.wait()
     cs[...] = sp[k] + pair[...]
     copies = [
@@ -197,34 +204,26 @@
     s_all = sall[...].reshape(256, 320)
     gp[...] = dot(s_all, s_all, 1, 1).reshape(16, 16, 256)
     copies = []
-    for i, (a, b) in enumerate(XY):
+    for i, (a, b) in enumerate(BALANCED):
         to_row = ((x + a) % 4) * 4 + (y + b) % 4
         copies.append(send(gp.at[to_row], grs.at[i], hs_sem.at[i], hr_sem.at[i], moved(a, b)))
+    right_copies = []
+    for h in range(2):
+        part[h] = dot(sall[h].reshape(128, 320), acc[...], 1, 0).reshape(16, 8, 800)
+        right_copies.append([])
+        for i, (a, b) in enumerate(BALANCED):
+            to_row = ((x + a) % 4) * 4 + (y + b) % 4
+            right_copies[h].append(
+                send(part.at[h, to_row], brs.at[h, i], bs_sem.at[h, i], br_sem.at[h, i], moved(a, b))
+            )
     total = gp[row]
     for i in range(15):
         copies[i].wait_recv()
         total = total + grs[i]
     gall2[row] = total
     sent += copies
-    for i, (a, b) in enumerate(XY):
+    for i, (a, b) in enumerate(BALANCED):
         sent.append(send(gall2.at[row], gall2.at[row], ts_sem.at[i], tr_sem.at[row], moved(a, b)))
-    for a, b in XY:
-        owner = ((x + 4 - a) % 4) * 4 + (y + 4 - b) % 4
-        landed(gall2.at[owner], tr_sem.at[owner], ts_sem.at[0])
-
-    ah[:, 0:256] = gall2[...].reshape(256, 256)
-    ah[:, 256:576] = s_all
-    right_copies = []
-    for h in range(2):
-        orthonormal((2 * h, 2 * h + 1), bt, ah)
-        part[h] = dot(bt[128 * h : 128 * h + 128, :], acc[...], 1, 0).reshape(16, 8, 800)
-        right_copies.append([])
-        for i, (a, b) in enumerate(BALANCED):
-            to_row = ((x + a) % 4) * 4 + (y + b) % 4
-            right_copies[h].append(
-                send(part.at[h, to_row], brs.at[h, i], bs_sem.at[h, i], br_sem.at[h, i], moved(a, b))
-            )
-    sums = []
     for h in range(2):
         total = part[h, row]
         for i in range(15):
@@ -232,40 +231,38 @@
             total = total + brs[h, i]
         sent += right_copies[h]
         rall[h, row] = total
-        sums.append(jnp.sum(total * total, axis=1, keepdims=True))
-        if h == 1:
-            diagonal = lax.broadcasted_iota(jnp.int32, (16, 128), 0) == lax.broadcasted_iota(jnp.int32, (16, 128), 1)
-            squares = jnp.concatenate(sums, axis=0)
-            sq[...] = jnp.sum(jnp.where(diagonal, squares, 0.0), axis=0, keepdims=True)
-            c = send(sq, sq2, qp_sem.at[0], qp_sem.at[1], moved(0, 0, 0, 1))
         for i, (a, b) in enumerate(BALANCED):
             sent.append(send(rall.at[h, row], rall.at[h, row], cs_sem.at[h, i], cr_sem.at[h, row], moved(a, b)))
+    for a, b in XY:
+        owner = ((x + 4 - a) % 4) * 4 + (y + 4 - b) % 4
+        landed(gall2.at[owner], tr_sem.at[owner], ts_sem.at[0])
+
+    inverse = factor_inverse(gall2[...].reshape(256, 256), ah)
+    basis_out[...] = dot(inverse, s_all, 1, 0).T
+    for h in range(2):
+        for a, b in XY:
+            owner = ((x + 4 - a) % 4) * 4 + (y + 4 - b) % 4
+            landed(rall.at[h, owner], cr_sem.at[h, owner], cs_sem.at[0, 0])
+    right = dot(inverse, rall[...].reshape(256, 800), 1, 0)
+
+    diagonal = lax.broadcasted_iota(jnp.int32, (128, 128), 0) == lax.broadcasted_iota(jnp.int32, (128, 128), 1)
+    squares = jnp.sum(right * right, axis=1, keepdims=True)
+    for h in range(2):
+        line = jnp.where(diagonal, squares[128 * h : 128 * h + 128], 0.0)
+        sq[:, 128 * h : 128 * h + 128] = jnp.sum(line, axis=0, keepdims=True)
+    c = send(sq, sq2, qp_sem.at[0], qp_sem.at[1], moved(0, 0, 0, 1))
     c.wait()
     sq[...] = sq[...] + sq2[...]
     copies = [send(sq, sqs.at[d], qs_sem.at[d], qr_sem.at[d], moved(0, 0, d)) for d in NEAR_Z[::-1]]
-    high_ref[...], low_ref[...] = halves(bt[...].T)
+    high_ref[...], low_ref[...] = halves(right)
+    right_out[...] = right.T
     total = sq[...]
     for i in range(15):
         copies[14 - i].wait_recv()
         total = total + sqs[NEAR_Z[i]]
     sent += copies
-    sqall[row] = total
-    for i, (a, b) in enumerate(BALANCED):
-        sent.append(send(sqall.at[row], sqall.at[row], us_sem.at[i], ur_sem.at[row], moved(a, b)))
-    for h in range(2):
-        for a, b in XY:
-            owner = ((x + 4 - a) % 4) * 4 + (y + 4 - b) % 4
-            landed(rall.at[h, owner], cr_sem.at[h, owner], cs_sem.at[0, 0])
-        right_out[128 * h : 128 * h + 128, :] = rall[h].reshape(128, 800)
-    for a, b in XY:
-        owner = ((x + 4 - a) % 4) * 4 + (y + 4 - b) % 4
-        landed(sqall.at[owner], ur_sem.at[owner], us_sem.at[0])
-    lane = lax.broadcasted_iota(jnp.int32, (16, 8, 128), 2)
-    line = lax.broadcasted_iota(jnp.int32, (16, 8, 128), 1)
-    rows = jnp.broadcast_to(sqall[...], (16, 8, 128))
-    for h in range(2):
-        squares = jnp.sum(jnp.where(lane == line + 8 * h, rows, 0.0), axis=2, keepdims=True)
-        squares_out[128 * h : 128 * h + 128, :] = jnp.broadcast_to(squares.reshape(128, 1), (128, 128))
+    squares_out[...] = total
+    moment_copy.wait()
     for c in sent:
         c.wait_send()
 
@@ -288,52 +285,52 @@
             line = wide(rows[p][j : j + 1])
             for t in range(p, 8):
                 factor = col[t][j] * inverse
+                for i in range(j + 1, 8):
+                    col[t][i] = col[t][i] - factor * b[i]
                 if t == p:
                     factor = jnp.where(sub > j, factor, 0.0)
-                for i in range(j + 1, 8):
-                    col[t][i] = col[t][i] - factor * b[i]
                 rows[t] = rows[t] - factor * line
         rows[p] = rows[p] * lax.rsqrt(pivots)
     return jnp.concatenate(rows, axis=0)
 
 
-def orthonormal(blocks, bt_ref, ah):
+def factor_inverse(gram, ah):
+    ah[:, 0:256] = gram
+    lines = lax.broadcasted_iota(jnp.int32, (256, 256), 0)
+    ah[:, 256:512] = jnp.where(lines == lax.broadcasted_iota(jnp.int32, (256, 256), 1), 1.0, 0.0)
+    done = []
     lane = lax.broadcasted_iota(jnp.int32, (64, 128), 1)
     line = lax.broadcasted_iota(jnp.int32, (64, 128), 0)
-    for b in blocks:
+    for b in range(4):
         parity, low = b % 2, 64 * b
         own = (lane // 64) == parity
         unit = jnp.where(lane == line + 64 * (1 - parity), 1.0, 0.0)
         tile = jnp.where(own, ah[low : low + 64, 128 * (b // 2) : 128 * (b // 2) + 128], unit)
         inverse = jnp.where(own, 0.0, factor_64(tile, parity))
         first = 128 * ((b + 1) // 2)
-        block = ah[low : low + 64, first:576]
+        block = ah[low : low + 64, first:512]
         upper = dot(inverse, jnp.concatenate([block, block], axis=0), 1, 0)
-        bt_ref[low : low + 64, :] = upper[:, 256 - first :]
+        done.append(upper[:, 256 - first :])
         if b < 3:
             change = dot(upper[:, : 256 - first], upper, 0, 0)
-            ah[low + 64 : 256, first:576] = ah[low + 64 : 256, first:576] - change[low + 64 - first :, :]
-
-
-def update_kernel(w_ref, moment_ref, high_ref, low_ref, right_ref, squares_ref, w_out, m_out, f_out, terms):
-    @pl.when(pl.program_id(0) == 0)
-    def _():
-        right = right_ref[...]
-        factor = right * lax.rsqrt(squares_ref[...][:, :1] / N + tiny_eps)
-        f_out[...] = factor.T
-        terms[0], terms[1] = halves(right)
-        terms[2], terms[3] = halves(factor)
-
-    high, low = high_ref[...], low_ref[...]
-
-    def product(first, second):
-        rest = dot_bf16(high, terms[second], 1, 0) + dot_bf16(low, terms[first], 1, 0)
-        return dot_bf16(high, terms[first], 1, 0) + rest
-
-    m_out[...] = moment_ref[...] - (1.0 - mix_rate) * product(0, 1)
+            ah[low + 64 : 256, first:512] = ah[low + 64 : 256, first:512] - change[low + 64 - first :, :]
+    return jnp.concatenate(done, axis=0)
+
+
+def update_kernel(w_ref, moment_ref, basis_ref, high_ref, low_ref, right_ref, squares_ref, w_out, m_out, f_out):
+    scale = lax.rsqrt(squares_ref[...] / N + tiny_eps)
+    f_out[...] = right_ref[...] * scale
+
+    def product(left):
+        high, low = halves(left)
+        rest = dot_bf16(high, low_ref[...], 1, 0) + dot_bf16(low, high_ref[...], 1, 0)
+        return dot_bf16(high, high_ref[...], 1, 0) + rest
+
+    basis = basis_ref[...]
+    m_out[...] = moment_ref[...] - (1.0 - mix_rate) * product(basis)
     w_out[...] = w_ref[...].astype(f32) * (1.0 - step_rate * weight_decay) - step_rate * math.sqrt(
         M / RANK
-    ) * product(2, 3)
+    ) * product(basis * scale)
 
 
 def vmem(count):
@@ -346,18 +343,19 @@
 
 def on_device(inputs, out_grads, weights, momentum, right_factor):
     dma = pltpu.SemaphoreType.DMA
-    moment, high, low, right, squares = pl.pallas_call(
+    moment, basis, high, low, right, squares = pl.pallas_call(
         step_kernel,
         name="step",
         out_shape=(
             shape(320, 800),
-            jax.ShapeDtypeStruct((320, 256), bf16),
-            jax.ShapeDtypeStruct((320, 256), bf16),
-            shape(256, 800),
-            shape(256, 128),
+            shape(320, 256),
+            jax.ShapeDtypeStruct((256, 800), bf16),
+            jax.ShapeDtypeStruct((256, 800), bf16),
+            shape(800, 256),
+            shape(1, 256),
         ),
-        in_specs=vmem(4),
-        out_specs=tuple(vmem(5)),
+        in_specs=vmem(2) + [pl.BlockSpec(memory_space=pl.ANY)] + vmem(1),
+        out_specs=(pl.BlockSpec(memory_space=pl.ANY), *vmem(5)),
         scratch_shapes=[
             pltpu.VMEM((16, 800, 128), bf16),
             pltpu.VMEM((16, 2, 64, 320), bf16),
@@ -371,20 +369,18 @@
             pltpu.VMEM((16, 16, 256), f32),
             pltpu.VMEM((15, 16, 256), f32),
             pltpu.VMEM((16, 16, 256), f32),
-            pltpu.VMEM((256, 576), f32),
-            pltpu.VMEM((256, 320), f32),
+            pltpu.VMEM((256, 512), f32),
             pltpu.VMEM((2, 16, 8, 800), f32),
             pltpu.VMEM((2, 15, 8, 800), f32),
             pltpu.VMEM((2, 16, 8, 800), f32),
-            pltpu.VMEM((1, 128), f32),
-            pltpu.VMEM((1, 128), f32),
-            pltpu.VMEM((16, 1, 128), f32),
-            pltpu.VMEM((16, 1, 128), f32),
-            dma((2,)), dma((30,)), dma((16,)), dma((16,)), dma((18,)), dma((16,)), dma((16,)), dma((16,)),
+            pltpu.VMEM((1, 256), f32),
+            pltpu.VMEM((1, 256), f32),
+            pltpu.VMEM((16, 1, 256), f32),
+            dma((4,)), dma((30,)), dma((16,)), dma((16,)), dma((18,)), dma((16,)), dma((16,)), dma((16,)),
             dma((2,)), dma((16,)), dma((16,)), dma((16,)), dma((16,)), dma((16,)), dma((16,)),
             dma((15,)), dma((15,)), dma((15,)), dma((16,)),
             dma((2, 15)), dma((2, 15)), dma((2, 15)), dma((2, 16)),
-            dma((2,)), dma((16,)), dma((16,)), dma((15,)), dma((16,)),
+            dma((2,)), dma((16,)), dma((16,)),
         ],
         compiler_params=pltpu.CompilerParams(collective_id=0, has_side_effects=True, vmem_limit_bytes=VMEM_LIMIT),
     )(inputs.T, out_grads, momentum, right_factor)
@@ -399,18 +395,18 @@
                 pl.BlockSpec((80, 800), lines),
                 pl.BlockSpec((80, 800), lines),
                 pl.BlockSpec((80, 256), lines),
-                pl.BlockSpec((80, 256), lines),
                 pl.BlockSpec((256, 800), whole),
-                pl.BlockSpec((256, 128), whole),
+                pl.BlockSpec((256, 800), whole),
+                pl.BlockSpec((200, 256), lines),
+                pl.BlockSpec((1, 256), whole),
             ],
             out_specs=(
                 pl.BlockSpec((80, 800), lines),
                 pl.BlockSpec((80, 800), lines),
-                pl.BlockSpec((800, 256), whole),
+                pl.BlockSpec((200, 256), lines),
             ),
-            scratch_shapes=[pltpu.VMEM((4, 256, 800), bf16)],
             compiler_params=pltpu.CompilerParams(vmem_limit_bytes=VMEM_LIMIT),
-        )(weights, moment, high, low, right, squares)
+        )(weights, moment, basis, high, low, right, squares)
     )
 
 

time: 130 us -> 123 us (0.946)
  Pallas kernels: 129 us -> 122 us
    pallas_call x1, Pallas kernels: 123 us -> 116 us  [on_device(): pl.pallas_call(step_kernel, name='step', out_shape=(shape(320, 800), shap...]
where the time goes in v4:
time: 123 us; the launch traced here: 122 us
  Pallas kernels  122 us (99%)
    pallas_call x1, Pallas kernels, on_device(): pl.pallas_call(step_kernel, name='step', out_shape=(shape(320, 800), shap...  116 us
    pallas_call x1, Pallas kernels, on_device(): pl.pallas_call(update_kernel, name='updates', grid=(4,), out_shape=(shape...  5.31 us

profile of v4, /device:TPU:1, one launch (start us, length us, event | category | flops | bytes accessed | tf_op | source)
XLA Modules:
  0.0 122.4 jit_solution(679589180849958689)
XLA Ops:
  0.6 116.4 %step.1 = (f32[320,800]{1,0:T(8,128)}, f32[320,256]{1,0:T(8,128)}, bf16[256,800]{1,0:T(8,128)(2,1)}, bf16[256,800]{1,0:T(8,128)(2,1)}, f32[800,256]{1,0:T(8,128)}, /*index=5*/f32[1,256]{1,0:T(1,128)}) custom-call(bf16[800,128]{1,0:T(8,128)(2,1)} %bitcast.1, bf16[64,320]{1,0:T(8,128)(2,1)} %g_ref.1, f32[320,800]{1,0:T(8,128)} %m_ref.1, f32[800,256]{1,0:T(8,128)} %r_ref.1), custom_call_target="tpu_custom_call" | custom-call | tf_op jit(solution)/shard_map/step/pallas_call | solution.py:346
  117.0 5.3 %updates.1 = (f32[320,800]{1,0:T(8,128)}, f32[320,800]{1,0:T(8,128)}, f32[800,256]{1,0:T(8,128)}) custom-call(bf16[320,800]{1,0:T(8,128)(2,1)} %w_ref.1, f32[320,800]{1,0:T(8,128)} %get-tuple-element.9.moment_ref, f32[320,256]{1,0:T(8,128)} %get-tuple-element.10.basis_ref, bf16[256,800]{1,0:T(8,128)(2,1)} %get-tuple-element.11.high_ref, ...), custom_call_target="tpu_custom_call" | custom-call | tf_op jit(solution)/shard_map/updates/pallas_call | solution.py:389

commit v5 on v4

--- a/solution.py
+++ b/solution.py
@@ -91,11 +91,7 @@
 ):
     x, y, z, k = place()
     row = x * 4 + y
-    ready = greet(
-        [(0, 0, d, 0) for d in NEAR_Z[::-1]]
-        + [(a, b, 0, 0) for a, b in XY[::-1]]
-        + [(0, 0, 0, 1)]
-    )
+    ready = greet([(d, 0, 0, 0) for d in (2, 1, 3)] + [(0, d, 0, 0) for d in (2, 1, 3)] + [(0, 0, d, 0) for d in (2, 14, 1, 15)] + [(0, 0, 0, 1)])
     own_x = pltpu.make_async_copy(x_ref, xall.at[row], own_sem.at[0])
     own_g = pltpu.make_async_copy(g_ref, gall.at[z, k], own_sem.at[1])
     own_m = pltpu.make_async_copy(m_ref, acc, own_sem.at[2])
@@ -133,16 +129,7 @@
     def cross_g(owner):
         sent.append(send(gall.at[owner, k], gall.at[owner, k], gd_sem.at[owner], gk_sem.at[owner], moved(0, 0, 0, 1)))
 
-    pass_g(z, (8, 4, 12))
-    for d in (1, 3, 2):
-        pass_on(0, row, True, (d,))
-        pass_on(1, row, False, (d,))
-    pass_g(z, (1, 15, 2))
-    cross_g(z)
-    for d in (1, 3, 2):
-        pass_on(0, row, False, (d,))
-        pass_on(1, row, True, (d,))
-    for d in (1, 3, 2):
+    def relay_x(d):
         ox = ((x + 4 - d) % 4) * 4 + y
         oy = x * 4 + (y + 4 - d) % 4
         landed(half(0, ox), xa_sem.at[ox], xs_sem.at[0])
@@ -150,16 +137,34 @@
         for e in (1, 3, 2):
             pass_on(0, ox, False, (e,))
             pass_on(1, oy, True, (e,))
-    for d in (4, 12, 8):
-        oz = (z + 16 - d) % 16
-        landed(gall.at[oz, k], gr_sem.at[oz], gs_sem.at[0])
-        pass_g(oz, (1, 15, 2))
-        cross_g(oz)
-    for a in (0, 4, 12, 8):
-        for d in (1, 15, 2):
-            oz = (z + 32 - d - a) % 16
-            landed(gall.at[oz, k], gr_sem.at[oz], gs_sem.at[0])
-            cross_g(oz)
+
+    def take_g(owner, ds):
+        landed(gall.at[owner, k], gr_sem.at[owner], gs_sem.at[0])
+        pass_g(owner, ds)
+        cross_g(owner)
+
+    def relay_g(d):
+        take_g((z + 16 - d) % 16, (2, 1))
+        take_g((z + d) % 16, (14, 15) if d < 6 else (15,))
+
+    pass_g(z, (2, 14, 1, 15))
+    for d in (1, 3, 2):
+        pass_on(0, row, True, (d,))
+        pass_on(1, row, False, (d,))
+    cross_g(z)
+    for d in (1, 3, 2):
+        pass_on(0, row, False, (d,))
+        pass_on(1, row, True, (d,))
+    relay_g(2)
+    relay_x(1)
+    relay_g(4)
+    relay_x(3)
+    relay_x(2)
+    relay_g(6)
+    for d in (1, 3, 5, 7):
+        take_g((z + 16 - d) % 16, ())
+        take_g((z + d) % 16, ())
+    take_g((z + 8) % 16, ())
     for i in range(16):
         landed(gall.at[i, 1 - k], gk_sem.at[i], gd_sem.at[0])
     for a, b in XY:

time: 123 us -> 116 us (0.943)
  Pallas kernels: 122 us -> 115 us
    pallas_call x1, Pallas kernels: 116 us -> 110 us  [on_device(): pl.pallas_call(step_kernel, name='step', out_shape=(shape(320, 800), shap...]
where the time goes in v5:
time: 116 us
  Pallas kernels  115 us (99%)
    pallas_call x1, Pallas kernels, on_device(): pl.pallas_call(step_kernel, name='step', out_shape=(shape(320, 800), shap...  110 us
    pallas_call x1, Pallas kernels, on_device(): pl.pallas_call(update_kernel, name='updates', grid=(4,), out_shape=(shape...  5.31 us

profile of v5, /device:TPU:1, one launch (start us, length us, event | category | flops | bytes accessed | tf_op | source)
XLA Modules:
  0.0 116.0 jit_solution(12219763439174496028)
XLA Ops:
  0.6 110.1 %step.1 = (f32[320,800]{1,0:T(8,128)}, f32[320,256]{1,0:T(8,128)}, bf16[256,800]{1,0:T(8,128)(2,1)}, bf16[256,800]{1,0:T(8,128)(2,1)}, f32[800,256]{1,0:T(8,128)}, /*index=5*/f32[1,256]{1,0:T(1,128)}) custom-call(bf16[800,128]{1,0:T(8,128)(2,1)} %bitcast.1, bf16[64,320]{1,0:T(8,128)(2,1)} %g_ref.1, f32[320,800]{1,0:T(8,128)} %m_ref.1, f32[800,256]{1,0:T(8,128)} %r_ref.1), custom_call_target="tpu_custom_call" | custom-call | tf_op jit(solution)/shard_map/step/pallas_call | solution.py:351
  110.7 5.3 %updates.1 = (f32[320,800]{1,0:T(8,128)}, f32[320,800]{1,0:T(8,128)}, f32[800,256]{1,0:T(8,128)}) custom-call(bf16[320,800]{1,0:T(8,128)(2,1)} %w_ref.1, f32[320,800]{1,0:T(8,128)} %get-tuple-element.9.moment_ref, f32[320,256]{1,0:T(8,128)} %get-tuple-element.10.basis_ref, bf16[256,800]{1,0:T(8,128)(2,1)} %get-tuple-element.11.high_ref, ...), custom_call_target="tpu_custom_call" | custom-call | tf_op jit(solution)/shard_map/updates/pallas_call | solution.py:394

commit v6 on v5

--- a/solution.py
+++ b/solution.py
@@ -83,7 +83,7 @@
 def step_kernel(
     x_ref, g_ref, m_ref, r_ref,
     moment_ref, basis_out, high_ref, low_ref, right_out, squares_out,
-    xall, gall, rt, acc, sp, pair, cs, rs, sall, gp, grs, gall2, ah,
+    xall, gall, gt, rt, acc, sp, pair, cs, rs, sall, gp, grs, gall2, ah,
     part, brs, rall, sq, sq2, sqs,
     own_sem, xs_sem, xa_sem, xb_sem, gs_sem, gr_sem, gd_sem, gk_sem,
     p_sem, zs_sem, zr_sem, as_sem, ar_sem, aks_sem, akr_sem, hs_sem, hr_sem, ts_sem, tr_sem,
@@ -108,7 +108,7 @@
     gnum = 0
 
     def half(which, owner):
-        return xall.at[owner, pl.ds(400 * which, 400)]
+        return xall.at[owner, pl.ds(384, 416)] if which else xall.at[owner, pl.ds(0, 384)]
 
     def pass_on(which, owner, along_x, ds):
         nonlocal number
@@ -167,16 +167,23 @@
     take_g((z + 8) % 16, ())
     for i in range(16):
         landed(gall.at[i, 1 - k], gk_sem.at[i], gd_sem.at[0])
-    for a, b in XY:
-        owner = ((x + 4 - a) % 4) * 4 + (y + 4 - b) % 4
-        if b != 0:
+
+    own_m.wait()
+    for i in range(16):
+        gt[i] = gall[i].reshape(128, 320).T
+    for d in (0, 1, 3, 2):
+        gx, gy = (x + 4 - d) % 4, (y + 4 - d) % 4
+        for e in (1, 3, 2):
+            owner = gx * 4 + (y + 4 - e) % 4
             landed(half(0, owner), xa_sem.at[owner], xs_sem.at[0])
-        if a != 0:
+            owner = ((x + 4 - e) % 4) * 4 + gy
             landed(half(1, owner), xb_sem.at[owner], xs_sem.at[0])
-
-    columns = jnp.concatenate([xall[i] for i in range(16)], axis=1)
-    own_m.wait()
-    acc[...] += dot_bf16(gall[...].reshape(2048, 320), columns, 0, 1)
+        left = jnp.concatenate([gt[gx * 4 + i] for i in range(4)], axis=1)
+        lines = jnp.concatenate([xall[gx * 4 + i, 0:384] for i in range(4)], axis=1)
+        acc[:, 0:384] += dot_bf16(left, lines, 1, 1)
+        left = jnp.concatenate([gt[i * 4 + gy] for i in range(4)], axis=1)
+        lines = jnp.concatenate([xall[i * 4 + gy, 384:800] for i in range(4)], axis=1)
+        acc[:, 384:800] += dot_bf16(left, lines, 1, 1)
     moment_copy = pltpu.make_async_copy(acc, moment_ref, own_sem.at[3])
     moment_copy.start()
     other = rt[pl.ds(pl.multiple_of(128 * (1 - k), 128), 128), :]
@@ -364,6 +371,7 @@
         scratch_shapes=[
             pltpu.VMEM((16, 800, 128), bf16),
             pltpu.VMEM((16, 2, 64, 320), bf16),
+            pltpu.VMEM((16, 320, 128), bf16),
             pltpu.VMEM((256, 800), f32),
             pltpu.VMEM((320, 800), f32),
             pltpu.VMEM((2, 16, 8, 320), f32),

time: 116 us -> 116 us (level)
  no operation moved by 1% of the time
where the time goes in v6:
time: 116 us
  Pallas kernels  115 us (99%)
    pallas_call x1, Pallas kernels, on_device(): pl.pallas_call(step_kernel, name='step', out_shape=(shape(320, 800), shap...  110 us
    pallas_call x1, Pallas kernels, on_device(): pl.pallas_call(update_kernel, name='updates', grid=(4,), out_shape=(shape...  5.32 us

profile of v6, /device:TPU:1, one launch (start us, length us, event | category | flops | bytes accessed | tf_op | source)
XLA Modules:
  0.0 115.6 jit_solution(2356896494683948410)
XLA Ops:
  0.6 109.6 %step.1 = (f32[320,800]{1,0:T(8,128)}, f32[320,256]{1,0:T(8,128)}, bf16[256,800]{1,0:T(8,128)(2,1)}, bf16[256,800]{1,0:T(8,128)(2,1)}, f32[800,256]{1,0:T(8,128)}, /*index=5*/f32[1,256]{1,0:T(1,128)}) custom-call(bf16[800,128]{1,0:T(8,128)(2,1)} %bitcast.1, bf16[64,320]{1,0:T(8,128)(2,1)} %g_ref.1, f32[320,800]{1,0:T(8,128)} %m_ref.1, f32[800,256]{1,0:T(8,128)} %r_ref.1), custom_call_target="tpu_custom_call" | custom-call | tf_op jit(solution)/shard_map/step/pallas_call | solution.py:358
  110.3 5.3 %updates.1 = (f32[320,800]{1,0:T(8,128)}, f32[320,800]{1,0:T(8,128)}, f32[800,256]{1,0:T(8,128)}) custom-call(bf16[320,800]{1,0:T(8,128)(2,1)} %w_ref.1, f32[320,800]{1,0:T(8,128)} %get-tuple-element.9.moment_ref, f32[320,256]{1,0:T(8,128)} %get-tuple-element.10.basis_ref, bf16[256,800]{1,0:T(8,128)(2,1)} %get-tuple-element.11.high_ref, ...), custom_call_target="tpu_custom_call" | custom-call | tf_op jit(solution)/shard_map/updates/pallas_call | solution.py:402
